TPU v7x, 256 devices: a whole 4x4x8 slice. The times are simulated.
256 devices in a mesh: kx: 8 (over x, z_lo), kyz: 32 (over z_hi, y, core).
Axes of the slice: x: 4, y: 4, z: 8 (z_hi: 4, z_lo: 2; z = z_hi * 2 + z_lo), core: 2. Of those that a mesh axis runs over, the one named last changes fastest.
Arguments:
- intersections: float32 [8, 32, 2, 2, 6, 2, 128, 128], P('kx', 'kyz'), may hold values from -1.2 to 1.2
- rotations: float32 [8, 32, 2, 2, 2, 128, 128], P('kx', 'kyz'), may hold values from -0.2 to 1.2
- offsets: int32 [6, 3], replicated, may hold values from -1 to 1, as said below
- weights: float32 [6], replicated, may hold values from 0.3 to 1.5
- basis: float32 [3, 3], replicated, may hold values from -3 to 3
Outputs:
- gradient: float32 [8, 32, 2, 2, 2, 128, 128], P('kx', 'kyz')
- centres: float32 [3, 128], replicated
- spread: float32 [], replicated
Inputs may be any that keep to these rules, and one draw needn't show every extreme that they name: `offsets`: each row is a step of -1, 0 or 1 along kx, ky and kz; no row is zero, no two rows are equal or opposite, and the unit steps along kx, ky and kz are among the rows.
All inputs are finite; a program needn't handle non-finite values.
Results may differ from a plain program's by a relative error of at most 0.0003.
Values sent between devices are 32-bit elements; how exact they have to be, the bound alone decides.
No kernel may reach another device: no remote copies, remote signals or barrier semaphores. Data moves between devices by JAX's collectives and lax.ppermute only.
A program may use at most 128 MiB of HBM per device.

v0:
```python
import functools

import jax
import jax.numpy as jnp
import numpy as np
from jax import lax
from jax.experimental import pallas as pl
from jax.experimental.pallas import tpu as pltpu
from jax.sharding import PartitionSpec as P

NB = 6
KZB = 4
J = 128
NKX = 8
NYZ = 32
NK = 1024
AXES = ("kx", "kyz")

UNITS = [(1, 0, 0), (0, 1, 0), (0, 0, 1)]
DIAGONALS = [
    (1, 1, 0),
    (1, -1, 0),
    (1, 0, 1),
    (1, 0, -1),
    (0, 1, 1),
    (0, 1, -1),
    (1, 1, 1),
    (1, 1, -1),
    (1, -1, 1),
    (1, -1, -1),
]
GRAY = [0, 1, 3, 2]
GROUPS = (
    [((0, 0, 0), t) for t in range(4)],
    [((1, 0, 0), t) for t in range(4)],
    [((0, 1, 0), 0), ((0, 1, 0), 1)],
    [((1, 1, 0), 0), ((1, 1, 0), 1), ((1, -1, 0), 2), ((1, -1, 0), 3)],
    [((0, 0, 1), 0), ((0, 0, 1), 2)],
    [((0, 1, 1), 0), ((1, 0, 1), 0), ((1, 0, 1), 2)],
    [((0, 0, -1), 3)],
    [((0, 1, -1), 1), ((1, 0, -1), 1), ((1, 0, -1), 3)],
    [((1, 1, 1), 0), ((1, -1, 1), 2)],
    [((1, 1, -1), 1), ((1, -1, -1), 3)],
)
SIZES = [len(group) for group in GROUPS]
SLOTS = sum(SIZES)
BACK = SIZES[:4] + [SIZES[4] + SIZES[5], SIZES[6] + SIZES[7]] + SIZES[8:]
SLOT_OF = {where: i for i, where in enumerate(sum(GROUPS, []))}


def place(step, k):
    row, col = k // 2 + step[1], k % 2 + step[2]
    return (step[0], row // 2, col // 2), (row % 2) * 2 + col % 2


def beside_device(device, delta):
    x, r = device // NYZ, device % NYZ
    x = (x + delta[0]) % NKX
    y = (r // 4 + delta[1]) % (NYZ // 4)
    g = (GRAY[r % 4] + delta[2]) % KZB
    return x * NYZ + y * 4 + GRAY[g]


def upper_slots(step):
    return [SLOT_OF[place(step, k)] for k in range(4)]


UNIT_SLOTS = [upper_slots(step) for step in UNITS]
TABLE = np.array([upper_slots(step) for step in DIAGONALS], np.int32)
CODES = np.array([(s[0] + 1) * 9 + (s[1] + 1) * 3 + s[2] + 1 for s in UNITS + DIAGONALS], np.int32)


def halves(x):
    hi = x.astype(jnp.bfloat16)
    return hi, (x - hi.astype(jnp.float32)).astype(jnp.bfloat16)


def three(a_hi, a_lo, b_hi, b_lo):
    def dot(a, b):
        return lax.dot_general(a, b, (((1,), (0,)), ((), ())), preferred_element_type=jnp.float32)

    return dot(a_hi, b_hi) + (dot(a_hi, b_lo) + dot(a_lo, b_hi))


VMEM = pl.BlockSpec(memory_space=pltpu.VMEM)
SMEM = pl.BlockSpec(memory_space=pltpu.SMEM)
PARAMS = pltpu.CompilerParams(vmem_limit_bytes=48 * 1024 * 1024)


def mats(n):
    return jax.ShapeDtypeStruct((n, 2, J, J), jnp.float32)


def reals(n):
    return jax.ShapeDtypeStruct((n, J, J), jnp.float32)


def block(ref_hi, ref_lo, at, re, im, sign):
    for ref, part_re, part_im in zip((ref_hi, ref_lo), halves(re), halves(im)):
        ref[at, :J, :J] = part_re
        ref[at, :J, J:] = part_im
        ref[at, J:, :J] = -part_im if sign > 0 else part_im
        ref[at, J:, J:] = part_re if sign > 0 else -part_re


def left_kernel(u_ref, m_ref, v_ref, b_hi, b_lo):
    a_hi, a_lo = halves(jnp.concatenate([u_ref[0, 0].T, u_ref[0, 1].T], 1))
    for j in range(NB):
        block(b_hi, b_lo, j % 2, m_ref[0, j, 0], m_ref[0, j, 1], -1)
        made = three(a_hi, a_lo, b_hi[j % 2], b_lo[j % 2])
        v_ref[0, j, 0] = made[:, :J]
        v_ref[0, j, 1] = made[:, J:]


def left_products(own_u, local_m):
    return pl.pallas_call(
        left_kernel,
        grid=(4,),
        in_specs=[
            pl.BlockSpec((1, 2, J, J), lambda k: (k, 0, 0, 0)),
            pl.BlockSpec((1, NB, 2, J, J), lambda k: (k, 0, 0, 0, 0)),
        ],
        out_specs=pl.BlockSpec((1, NB, 2, J, J), lambda k: (k, 0, 0, 0, 0)),
        scratch_shapes=[
            pltpu.VMEM((2, 2 * J, 2 * J), jnp.bfloat16),
            pltpu.VMEM((2, 2 * J, 2 * J), jnp.bfloat16),
        ],
        out_shape=jax.ShapeDtypeStruct((4, NB, 2, J, J), jnp.float32),
        compiler_params=PARAMS,
        cost_estimate=pl.CostEstimate(flops=1 << 32, bytes_accessed=8 << 20, transcendentals=0),
        name="left_products",
    )(own_u, local_m)


def write_pair(p_ref, d_ref, at, left_re, left_im, right_re, right_im, b_hi, b_lo):
    a_hi, a_lo = halves(jnp.concatenate([left_re, left_im], 1))
    slot = at % 2
    block(b_hi, b_lo, slot, right_re, right_im, 1)
    made = three(a_hi, a_lo, b_hi[slot], b_lo[slot])
    eye = lax.broadcasted_iota(jnp.int32, (J, J), 0) == lax.broadcasted_iota(jnp.int32, (J, J), 1)
    p_ref[at, 0] = made[:, :J]
    p_ref[at, 1] = made[:, J:]
    j, k = at // 4, at % 4
    d_ref[0, j, k : k + 1, :] = jnp.sum(jnp.where(eye, made[:, :J], 0.0), 0, keepdims=True)
    d_ref[1, j, k : k + 1, :] = jnp.sum(jnp.where(eye, made[:, J:], 0.0), 0, keepdims=True)


def write_phases(row_data, first, d_ref, phase_ref, sums):
    for j in range(3):
        d_re, d_im = d_ref[0, j], d_ref[1, j]
        phase = jnp.arctan2(d_im, d_re)
        phase_ref[j] = phase
        weight = row_data[first + j, 0]
        along = jnp.sum(phase, 0, keepdims=True) * weight
        for c in range(3):
            sums[c] = sums[c] + along * row_data[first + j, 1 + c]
        spread = 1.0 - d_re * d_re - d_im * d_im + phase * phase
        sums[3] = sums[3] + weight * jnp.sum(spread, 0, keepdims=True)
    return jnp.concatenate(sums, 0)


def unit_kernel(rows, row_data, own_ref, x_ref, y_ref, z_ref, v_ref, p_ref, d_ref, phase_ref, sum_ref, b_hi, b_lo):
    found = {i: (own_ref, i) for i in range(4)}
    for ref, slots in ((x_ref, UNIT_SLOTS[0]), (y_ref, UNIT_SLOTS[1][2:]), (z_ref, UNIT_SLOTS[2][1::2])):
        found.update({slot: (ref, i) for i, slot in enumerate(slots)})
    for p in range(12):
        j, k = p // 4, p % 4
        ref, i = found[UNIT_SLOTS[j][k]]
        row = rows[j]
        write_pair(p_ref, d_ref, p, v_ref[k, row, 0], v_ref[k, row, 1], ref[i, 0], ref[i, 1], b_hi, b_lo)
    sum_ref[...] = write_phases(row_data, 0, d_ref, phase_ref, [jnp.zeros((1, J), jnp.float32)] * 4)


def diagonal_kernel(ends, rows, row_data, so_far_ref, *refs, any_sign):
    parts, rest = refs[: len(SIZES)], refs[len(SIZES) :]
    if any_sign:
        v_ref, far_ref, *rest = rest
    else:
        v_ref, *rest = rest
    p_ref, d_ref, phase_ref, sum_ref, slots, b_hi, b_lo = rest
    at = 0
    for ref, n in zip(parts, SIZES):
        slots[at : at + n] = ref[...]
        at += n
    for p in range(12):
        j, k = p // 4, p % 4
        low, up = ends[0, j, k], ends[1, j, k]
        if any_sign:
            left_re, left_im = far_ref[low, j, 0], far_ref[low, j, 1]
        else:
            row = rows[3 + j]
            left_re, left_im = v_ref[k, row, 0], v_ref[k, row, 1]
        write_pair(p_ref, d_ref, p, left_re, left_im, slots[up, 0], slots[up, 1], b_hi, b_lo)
    total = write_phases(row_data, 3, d_ref, phase_ref, [so_far_ref[i : i + 1] for i in range(4)])
    for i in range(NKX):
        sum_ref[i] = total


def product_call(kernel, name, tables, arrays, sum_shape, extra=()):
    return pl.pallas_call(
        kernel,
        in_specs=[SMEM] * len(tables) + [VMEM] * len(arrays),
        out_specs=[VMEM] * 4,
        out_shape=[mats(12)] + [jax.ShapeDtypeStruct(n + (J,), jnp.float32) for n in ((2, 3, 4), (3, 4), sum_shape)],
        scratch_shapes=[
            *extra,
            pltpu.VMEM((2, 2 * J, 2 * J), jnp.bfloat16),
            pltpu.VMEM((2, 2 * J, 2 * J), jnp.bfloat16),
        ],
        compiler_params=PARAMS,
        cost_estimate=pl.CostEstimate(flops=1 << 32, bytes_accessed=4 << 20, transcendentals=0),
        name=name,
    )(*tables, *arrays)


def unit_products(rows, row_data, own, x, y, z, v):
    return product_call(unit_kernel, "unit_products", [rows, row_data], [own, x, y, z, v], (4,))


def diagonal_products(ends, rows, row_data, so_far, parts, v, far=None):
    return product_call(
        functools.partial(diagonal_kernel, any_sign=far is not None),
        "diagonal_products",
        [ends, rows, row_data],
        [so_far, *parts, v] + ([] if far is None else [far]),
        (NKX, 4),
        [pltpu.VMEM((SLOTS, 2, J, J), jnp.float32)],
    )


def plain_and_cross(re, im, a, b):
    return re * a + im * b, im * a - re * b


def term_kernel(ends, row_data, pu_ref, du_ref, phu_ref, pd_ref, dd_ref, phd_ref, got_ref, *refs):
    total_ref, outs = refs[0], refs[1 : 1 + len(BACK)]
    plain, cross, rows_a, rows_b, turned_a, turned_b = refs[1 + len(BACK) :]
    total = jnp.sum(got_ref[...], 0)
    total_ref[...] = total
    centres = (-2.0 / NK) * total[:3]
    for j in range(NB):
        along = centres[0:1] * row_data[j, 1]
        for c in range(1, 3):
            along += centres[c : c + 1] * row_data[j, 1 + c]
        d_ref, phase_ref = (du_ref, phu_ref) if j < 3 else (dd_ref, phd_ref)
        d_re, d_im = d_ref[0, j % 3], d_ref[1, j % 3]
        ratio = (phase_ref[j % 3] + along) / (d_re * d_re + d_im * d_im)
        f_re = row_data[j, 0] * (d_re + ratio * d_im)
        f_im = row_data[j, 0] * (ratio * d_re - d_im)
        rows_a[4 * j : 4 * j + 4, :] = f_re + f_im
        rows_b[4 * j : 4 * j + 4, :] = f_re - f_im
    turned_a[...] = rows_a[...].T
    turned_b[...] = rows_b[...].T

    fixed = {slot: [] for slot in range(SLOTS)}
    for p in range(12):
        fixed[p % 4].append((p, True))
        fixed[UNIT_SLOTS[p // 4][p % 4]].append((p, False))
    step = J // 4
    for slot in range(SLOTS):
        for start in range(0, J, step):
            part = slice(start, start + step)
            sums = [jnp.zeros((step, J), jnp.float32)] * 2
            for p, starts_here in fixed[slot]:
                re, im = pu_ref[p, 0, part, :], pu_ref[p, 1, part, :]
                if starts_here:
                    a, b = rows_a[p : p + 1, :], rows_b[p : p + 1, :]
                    one, two = plain_and_cross(re, im, a, b)
                    sums = [sums[0] + one, sums[1] + two]
                else:
                    a, b = turned_a[part, p : p + 1], turned_b[part, p : p + 1]
                    one, two = plain_and_cross(re, im, a, b)
                    sums = [sums[0] - one, sums[1] - two]
            plain[slot, part, :], cross[slot, part, :] = sums
    for p in range(12):
        low, up = ends[0, p // 4, p % 4], ends[1, p // 4, p % 4]
        q = 12 + p
        for start in range(0, J, step):
            part = slice(start, start + step)
            re, im = pd_ref[p, 0, part, :], pd_ref[p, 1, part, :]
            one, two = plain_and_cross(re, im, rows_a[q : q + 1, :], rows_b[q : q + 1, :])
            plain[low, part, :] += one
            cross[low, part, :] += two
            one, two = plain_and_cross(re, im, turned_a[part, q : q + 1], turned_b[part, q : q + 1])
            plain[up, part, :] -= one
            cross[up, part, :] -= two
    at = 0
    for ref, n in zip(outs, BACK):
        for i in range(n):
            ref[i] = 2.0 * (plain[at] + cross[at].T)
            at += 1


def pair_terms(ends, row_data, unit, diagonal, got):
    return pl.pallas_call(
        term_kernel,
        in_specs=[SMEM, SMEM] + [VMEM] * 7,
        out_specs=[VMEM] * (1 + len(BACK)),
        out_shape=[jax.ShapeDtypeStruct((4, J), jnp.float32)] + [reals(n) for n in BACK],
        scratch_shapes=[pltpu.VMEM((SLOTS, J, J), jnp.float32)] * 2 + [pltpu.VMEM((J, J), jnp.float32)] * 4,
        compiler_params=PARAMS,
        cost_estimate=pl.CostEstimate(flops=1 << 24, bytes_accessed=8 << 20, transcendentals=0),
        name="pair_terms",
    )(ends, row_data, *unit, *diagonal, got)


def fold_kernel(own_ref, x_ref, y_ref, y_back_ref, z_ref, z_back_ref, g_ref):
    for k in range(4):
        total = own_ref[k] + x_ref[k]
        total += y_ref[k] if k < 2 else y_back_ref[k - 2]
        if k % 2 == 0:
            total += z_ref[k // 2]
        if k == 3:
            total += z_back_ref[0]
        turned = total.T
        g_ref[k, 0] = 0.5 * (total - turned)
        g_ref[k, 1] = 0.5 * (total + turned)


def fold_terms(*arrays):
    return pl.pallas_call(
        fold_kernel,
        in_specs=[VMEM] * len(arrays),
        out_specs=VMEM,
        out_shape=mats(4),
        compiler_params=PARAMS,
        name="fold_terms",
    )(*arrays)


def fetch(delta, *blocks):
    route = [(beside_device(i, delta), i) for i in range(NKX * NYZ)]
    return lax.ppermute(jnp.concatenate(blocks, 0), AXES, route)


def give_back(delta, block):
    route = [(i, beside_device(i, delta)) for i in range(NKX * NYZ)]
    return lax.ppermute(block, AXES, route)


X, Y, Y_BACK, Z, Z_BACK = (1, 0, 0), (0, 1, 0), (0, -1, 0), (0, 0, 1), (0, 0, -1)


def halo(own):
    y = fetch(Y, own[0:2])
    y_back = fetch(Y_BACK, own[2:4])
    x = fetch(X, own)
    z = fetch(Z, own[0::2])
    z_back = fetch(Z_BACK, own[3:4])
    xy = fetch(X, y, y_back)
    beside = fetch(Z, y[0:1], x[0::2])
    beside_back = fetch(Z_BACK, y[1:2], x[1::2])
    corner = fetch(Z, xy[0::2])
    corner_back = fetch(Z_BACK, xy[1::2])
    return own, x, y, xy, z, beside, z_back, beside_back, corner, corner_back


def fold_halo(own, x, y, xy, z, z_back, corner, corner_back):
    corner = give_back(Z, corner)
    corner_back = give_back(Z_BACK, corner_back)
    z = give_back(Z, z)
    z_back = give_back(Z_BACK, z_back)
    corners = [corner[0:1], corner_back[0:1], corner[1:2], corner_back[1:2]]
    xy = give_back(X, xy + jnp.concatenate(corners, 0))
    sides = [z[3:4], z_back[2:3], z[4:5], z_back[3:4]]
    x = give_back(X, x + jnp.concatenate(sides, 0))
    y = give_back(Y, y + xy[0:2] + jnp.concatenate([z[2:3], z_back[1:2]], 0))
    y_back = give_back(Y_BACK, xy[2:4])
    return fold_terms(own, x, y, y_back, z, z_back)


def over_all(copies):
    x = jnp.sum(lax.all_to_all(copies, "kx", 0, 0), 0)
    return lax.all_to_all(jnp.broadcast_to(x[None], (NYZ,) + x.shape), "kyz", 0, 0)


def on_device(intersections, rotations, offsets, weights, basis):
    own_u = rotations.reshape(4, 2, J, J)
    local_m = intersections.reshape(4, NB, 2, J, J)
    parts = halo(own_u)
    v = left_products(own_u, local_m)

    code = (offsets[:, 0] + 1) * 9 + (offsets[:, 1] + 1) * 3 + offsets[:, 2] + 1
    with_sign = jnp.asarray(CODES)[:, None] == code[None, :]
    against = 26 - jnp.asarray(CODES)[:, None] == code[None, :]
    here = with_sign | against
    rank = jnp.cumsum(jnp.any(here[3:], 1).astype(jnp.int32))
    nth = (rank[None] == jnp.arange(1, 4, dtype=jnp.int32)[:, None])[:, :, None] & here[None, 3:]
    chosen = jnp.concatenate([here[:3], jnp.any(nth, 1)], 0)
    rows = jnp.sum(jnp.where(chosen, jnp.arange(NB, dtype=jnp.int32)[None], 0), 1)
    upper = jnp.sum(jnp.where(jnp.any(nth, 2)[:, :, None], jnp.asarray(TABLE), 0), 1)
    lower = jnp.broadcast_to(jnp.arange(4, dtype=jnp.int32)[None], (3, 4))
    flipped = jnp.any(nth & against[None, 3:], (1, 2))
    ends = jnp.stack(
        [jnp.where(flipped[:, None], upper, lower), jnp.where(flipped[:, None], lower, upper)]
    )
    step_vec = jnp.sum(offsets.astype(jnp.float32)[:, :, None] * basis[None], 1)
    row_data = jnp.concatenate([weights[:, None], step_vec], 1)
    row_data = jnp.sum(jnp.where(chosen[:, :, None], row_data[None], 0.0), 1)

    *unit, so_far = unit_products(rows, row_data, own_u, parts[1], parts[2], parts[4], v)

    def usual(ends, rows, row_data, so_far, v, *parts):
        return diagonal_products(ends, rows, row_data, so_far, parts, v)

    def any_sign(ends, rows, row_data, so_far, v, *parts):
        far = halo(jnp.stack([v[:, rows[j]] for j in range(3, NB)], 1))
        return diagonal_products(ends, rows, row_data, so_far, parts, v, jnp.concatenate(far, 0))

    *diagonal, part = lax.cond(
        jnp.any(flipped), any_sign, usual, ends, rows, row_data, so_far, v, *parts
    )
    got = over_all(part)
    total, *terms = pair_terms(ends, row_data, unit, diagonal, got)
    gradient = fold_halo(*terms)
    centres = (-2.0 / NK) * total[:3]
    spread = (2.0 / NK) * jnp.sum(total[3]) - jnp.sum(centres * centres)
    return gradient.reshape(1, 1, 2, 2, 2, J, J), centres, spread


def solution(mesh):
    placed = (
        P("kx", "kyz", None, None, None, None, None, None),
        P("kx", "kyz", None, None, None, None, None),
        P(),
        P(),
        P(),
    )
    return jax.shard_map(
        on_device,
        mesh=mesh,
        in_specs=placed,
        out_specs=(P("kx", "kyz", None, None, None, None, None), P(), P()),
        check_vma=False,
    )
```

profile of v0, /device:TPU:1, one launch (start us, length us, event | category | flops | bytes accessed | tf_op | source)
XLA Modules:
  0.0 122.0 jit_solution(17325673864194452174)
XLA Ops:
  0.6 4.7 %collective-permute-start.10 = (f32[4,2,128,128]{3,2,1,0:T(8,128)}, f32[4,2,128,128]{3,2,1,0:T(8,128)S(1)}, u32[]{:S(2)}, u32[]{:S(2)}) collective-permute-start(f32[4,2,128,128]{3,2,1,0:T(8,128)} %bitcast.20), channel_id=1, source_target_pairs={{32,0},{33,1},{34,2},{35,3},{36,4},{37,5},{38,6},{39,7},{40,8},{41... | collective-permute-start | bytes 1572872 | tf_op jit(solution)/shard_map/ppermute | solution.py:333
  5.4 1.6 %slice.177 = f32[1,2,128,128]{3,2,1,0:T(8,128)} slice(f32[4,2,128,128]{3,2,1,0:T(8,128)} %bitcast.21), slice={[3:4], [0:2], [0:128], [0:128]} | slice | bytes 262144 | tf_op jit(solution)/shard_map/slice | solution.py:349
  10.4 2.7 %collective-permute-start.13 = (f32[2,2,128,128]{3,2,1,0:T(8,128)S(1)}, f32[2,2,128,128]{3,2,1,0:T(8,128)S(1)}, u32[]{:S(2)}, u32[]{:S(2)}) collective-permute-start(f32[2,2,128,128]{3,2,1,0:T(8,128)S(1)} %get-tuple-element.154), channel_id=1, source_target_pairs={{28,0},{29,1},{30,2},{31,3},{0,4},{1,5},{2,6},{3,7},{4,8},{5,9},{6... | collective-permute-start | bytes 786440 | tf_op jit(solution)/shard_map/ppermute | solution.py:333
  13.1 4.9 %collective-permute-start.11 = (f32[2,2,128,128]{3,2,1,0:T(8,128)S(1)}, f32[2,2,128,128]{3,2,1,0:T(8,128)S(1)}, u32[]{:S(2)}, u32[]{:S(2)}) collective-permute-start(f32[2,2,128,128]{3,2,1,0:T(8,128)S(1)} %get-tuple-element.155), channel_id=1, source_target_pairs={{4,0},{5,1},{6,2},{7,3},{8,4},{9,5},{10,6},{11,7},{12,8},{13,9},{1... | collective-permute-start | bytes 786440 | tf_op jit(solution)/shard_map/ppermute | solution.py:333
  20.6 1.9 %copy-done = f32[1,1,2,2,6,2,128,128]{7,6,5,4,3,2,1,0:T(8,128)S(1)} copy-done((f32[1,1,2,2,6,2,128,128]{7,6,5,4,3,2,1,0:T(8,128)S(1)}, f32[1,1,2,2,6,2,128,128]{7,6,5,4,3,2,1,0:T(8,128)}, u32[]{:S(2)}) %copy-start) | copy-done | bytes 3145752
  22.5 5.0 %left_products.1.v_ref = f32[4,6,2,128,128]{4,3,2,1,0:T(8,128)} custom-call(f32[4,2,128,128]{3,2,1,0:T(8,128)} %bitcast.23, f32[4,6,2,128,128]{4,3,2,1,0:T(8,128)S(1)} %bitcast.19), custom_call_target="tpu_custom_call" | custom-call | flops 4294967296 | bytes 8388608 | tf_op jit(solution)/shard_map/left_products/pallas_call | solution.py:116
  29.7 6.1 %collective-permute-done.13 = f32[2,2,128,128]{3,2,1,0:T(8,128)S(1)} collective-permute-done((f32[2,2,128,128]{3,2,1,0:T(8,128)S(1)}, f32[2,2,128,128]{3,2,1,0:T(8,128)S(1)}, u32[]{:S(2)}, u32[]{:S(2)}) %collective-permute-start.13) | collective-permute-done | bytes 262176 | tf_op jit(solution)/shard_map/ppermute | solution.py:333
  36.1 2.1 %collective-permute-start.15 = (f32[3,2,128,128]{3,2,1,0:T(8,128)S(1)}, f32[3,2,128,128]{3,2,1,0:T(8,128)}, u32[]{:S(2)}, u32[]{:S(2)}) collective-permute-start(f32[3,2,128,128]{3,2,1,0:T(8,128)S(1)} %pad_maximum_fusion.5), channel_id=1, source_target_pairs={{1,0},{3,1},{0,2},{2,3},{5,4},{7,5},{4,6},{6,7},{9,8},{11,9},{8,10... | collective-permute-start | bytes 1179656 | tf_op jit(solution)/shard_map/ppermute | solution.py:333
  38.4 9.2 %collective-permute-done.14 = f32[4,2,128,128]{3,2,1,0:T(8,128)} collective-permute-done((f32[4,2,128,128]{3,2,1,0:T(8,128)S(1)}, f32[4,2,128,128]{3,2,1,0:T(8,128)}, u32[]{:S(2)}, u32[]{:S(2)}) %collective-permute-start.14) | collective-permute-done | bytes 524320 | tf_op jit(solution)/shard_map/ppermute | solution.py:333
  49.4 2.3 %collective-permute-start.18 = (f32[2,2,128,128]{3,2,1,0:T(8,128)S(1)}, f32[2,2,128,128]{3,2,1,0:T(8,128)}, u32[]{:S(2)}, u32[]{:S(2)}) collective-permute-start(f32[2,2,128,128]{3,2,1,0:T(8,128)S(1)} %get-tuple-element.151), channel_id=1, source_target_pairs={{1,0},{3,1},{0,2},{2,3},{5,4},{7,5},{4,6},{6,7},{9,8},{11,9},{8,10... | collective-permute-start | bytes 786440 | tf_op jit(solution)/shard_map/ppermute | solution.py:333
  51.7 3.3 %unit_products.1 = (f32[12,2,128,128]{3,2,1,0:T(8,128)S(1)}, f32[2,3,4,128]{3,2,1,0:T(4,128)S(1)}, f32[3,4,128]{2,1,0:T(4,128)S(1)}, f32[4,128]{1,0:T(4,128)S(1)}) custom-call(s32[6]{0:T(128)S(1)} %select_reduce_fusion.2.rows, f32[6,4]{1,0:T(8,128)S(1)} %select_reduce_fusion.row_data, f32[4,2,128,128]{3,2,1,0:T(8,128)S(1)} %bitcast.24, ...), custom_call_target="tpu_custom_call" | custom-call | flops 4294967296 | bytes 4194304 | tf_op jit(solution)/shard_map/unit_products/pallas_call | solution.py:200
  55.1 2.3 %collective-permute-done.18 = f32[2,2,128,128]{3,2,1,0:T(8,128)} collective-permute-done((f32[2,2,128,128]{3,2,1,0:T(8,128)S(1)}, f32[2,2,128,128]{3,2,1,0:T(8,128)}, u32[]{:S(2)}, u32[]{:S(2)}) %collective-permute-start.18) | collective-permute-done | bytes 262176 | tf_op jit(solution)/shard_map/ppermute | solution.py:333
  57.4 5.0 %conditional.1 = ((f32[12,2,128,128]{3,2,1,0:T(8,128)}, f32[2,3,4,128]{3,2,1,0:T(4,128)S(1)}, f32[3,4,128]{2,1,0:T(4,128)S(1)}, f32[8,4,128]{2,1,0:T(4,128)S(1)})) conditional(s32[]{:T(128)} %convert_element_type.25, (s32[2,3,4]{2,1,0:T(4,128)S(1)}, s32[6]{0:T(128)S(1)}, f32[6,4]{1,0:T(8,128)S(1)}, f32[4,128]{1,0:T(4,128)S(1)}, ...), branch_computations={%region_10.11_spmd, %region_11.12_spmd} | conditional | flops 4296736768 | bytes 140509856 | solution.py:410
  57.4 5.0 %diagonal_products.2 = (f32[12,2,128,128]{3,2,1,0:T(8,128)}, f32[2,3,4,128]{3,2,1,0:T(4,128)S(1)}, f32[3,4,128]{2,1,0:T(4,128)S(1)}, f32[8,4,128]{2,1,0:T(4,128)S(1)}) custom-call(s32[2,3,4]{2,1,0:T(4,128)S(1)} %get-tuple-element.60.ends, s32[6]{0:T(128)S(1)} %get-tuple-element.61.rows, f32[6,4]{1,0:T(8,128)S(1)} %get-tuple-element.62.row_data, ...), custom_call_target="tpu_custom_call" | custom-call | flops 4294967296 | bytes 4194304 | tf_op jit(solution)/shard_map/cond/branch_0_fun/diagonal_products/pallas_call | solution.py:200
  62.4 8.2 %all_to_all.10 = f32[8,4,128]{2,1,0:T(4,128)S(1)} all-to-all(f32[8,4,128]{2,1,0:T(4,128)S(1)} %get-tuple-element.117), channel_id=1, replica_groups=mesh['kx'=8,'kyz'=32] {'kx'}, dimensions={0} | all-to-all | bytes 32768 | tf_op jit(solution)/shard_map/all_to_all | solution.py:373
  70.7 18.9 %all_to_all.11.got_ref = f32[32,4,128]{2,1,0:T(4,128)S(1)} all-to-all(f32[32,4,128]{2,1,0:T(4,128)S(1)} %broadcast_in_dim.105), channel_id=1, replica_groups=mesh['kx'=8,'kyz'=32] {'kyz'}, dimensions={0} | all-to-all | bytes 131072 | tf_op jit(solution)/shard_map/all_to_all | solution.py:374
  89.5 3.4 %pair_terms.1 = (f32[4,128]{1,0:T(4,128)S(1)}, f32[4,128,128]{2,1,0:T(8,128)S(1)}, f32[4,128,128]{2,1,0:T(8,128)S(1)}, f32[2,128,128]{2,1,0:T(8,128)S(1)}, f32[4...) custom-call(s32[2,3,4]{2,1,0:T(4,128)S(1)} %pad_add_fusion.ends, ...), custom_call_target="tpu_custom_call" | custom-call | flops 16777216 | bytes 8388608 | tf_op jit(solution)/shard_map/pair_terms/pallas_call | solution.py:295
  93.5 1.9 %collective-permute-start.21 = (f32[4,128,128]{2,1,0:T(8,128)S(1)}, f32[4,128,128]{2,1,0:T(8,128)S(1)}, u32[]{:S(2)}, u32[]{:S(2)}) collective-permute-start(f32[4,128,128]{2,1,0:T(8,128)S(1)} %get-tuple-element.121), channel_id=1, source_target_pairs={{0,2},{1,0},{2,3},{3,1},{4,6},{5,4},{6,7},{7,5},{8,10},{9,8},{10,1... | collective-permute-start | bytes 786440 | tf_op jit(solution)/shard_map/ppermute | solution.py:338
  96.7 1.5 %collective-permute-done.24 = f32[2,128,128]{2,1,0:T(8,128)S(1)} collective-permute-done((f32[2,128,128]{2,1,0:T(8,128)S(1)}, f32[2,128,128]{2,1,0:T(8,128)S(1)}, u32[]{:S(2)}, u32[]{:S(2)}) %collective-permute-start.24) | collective-permute-done | bytes 131104 | tf_op jit(solution)/shard_map/ppermute | solution.py:338
  99.0 4.8 %collective-permute-done.21.z_back_ref = f32[4,128,128]{2,1,0:T(8,128)S(1)} collective-permute-done((f32[4,128,128]{2,1,0:T(8,128)S(1)}, f32[4,128,128]{2,1,0:T(8,128)S(1)}, u32[]{:S(2)}, u32[]{:S(2)}) %collective-permute-start.21) | collective-permute-done | bytes 262176 | tf_op jit(solution)/shard_map/ppermute | solution.py:338
  104.7 2.1 %collective-permute-done.25 = f32[4,128,128]{2,1,0:T(8,128)S(1)} collective-permute-done((f32[4,128,128]{2,1,0:T(8,128)S(1)}, f32[4,128,128]{2,1,0:T(8,128)S(1)}, u32[]{:S(2)}, u32[]{:S(2)}) %collective-permute-start.25) | collective-permute-done | bytes 262176 | tf_op jit(solution)/shard_map/ppermute | solution.py:338
  106.8 4.3 %collective-permute-start.27 = (f32[2,128,128]{2,1,0:T(8,128)S(1)}, f32[2,128,128]{2,1,0:T(8,128)S(1)}, u32[]{:S(2)}, u32[]{:S(2)}) collective-permute-start(f32[2,128,128]{2,1,0:T(8,128)S(1)} %get-tuple-element.159), channel_id=1, source_target_pairs={{0,28},{1,29},{2,30},{3,31},{4,0},{5,1},{6,2},{7,3},{8,4},{9,5},{1... | collective-permute-start | bytes 393224 | tf_op jit(solution)/shard_map/ppermute | solution.py:338
  113.0 2.4 %collective-permute-done.27.y_back_ref = f32[2,128,128]{2,1,0:T(8,128)S(1)} collective-permute-done((f32[2,128,128]{2,1,0:T(8,128)S(1)}, f32[2,128,128]{2,1,0:T(8,128)S(1)}, u32[]{:S(2)}, u32[]{:S(2)}) %collective-permute-start.27) | collective-permute-done | bytes 131104 | tf_op jit(solution)/shard_map/ppermute | solution.py:338
  115.5 4.5 %collective-permute-done.26.y_ref = f32[2,128,128]{2,1,0:T(8,128)S(1)} collective-permute-done((f32[2,128,128]{2,1,0:T(8,128)S(1)}, f32[2,128,128]{2,1,0:T(8,128)S(1)}, u32[]{:S(2)}, u32[]{:S(2)}) %collective-permute-start.26) | collective-permute-done | bytes 131104 | tf_op jit(solution)/shard_map/ppermute | solution.py:338
  (71 shorter events, 14.9 us)
Async XLA Ops:
  0.6 35.4 %collective-permute-start.10 = (f32[4,2,128,128]{3,2,1,0:T(8,128)}, f32[4,2,128,128]{3,2,1,0:T(8,128)S(1)}, u32[]{:S(2)}, u32[]{:S(2)}) collective-permute-start(f32[4,2,128,128]{3,2,1,0:T(8,128)} %bitcast.20), channel_id=1, source_target_pairs={{32,0},{33,1},{34,2},{35,3},{36,4},{37,5},{38,6},{39,7},{40,8},{41... | collective-permute-start | bytes 1572872 | tf_op jit(solution)/shard_map/ppermute | solution.py:333
  7.0 48.1 %collective-permute-start.16 = (f32[1,2,128,128]{3,2,1,0:T(8,128)}, f32[1,2,128,128]{3,2,1,0:T(8,128)S(1)}, u32[]{:S(2)}, u32[]{:S(2)}) collective-permute-start(f32[1,2,128,128]{3,2,1,0:T(8,128)} %slice.177), channel_id=1, source_target_pairs={{2,0},{0,1},{3,2},{1,3},{6,4},{4,5},{7,6},{5,7},{10,8},{8,9},{11,1... | collective-permute-start | bytes 393224 | tf_op jit(solution)/shard_map/ppermute | solution.py:333
  9.2 40.2 %collective-permute-start.12 = (f32[2,2,128,128]{3,2,1,0:T(8,128)S(1)}, f32[2,2,128,128]{3,2,1,0:T(8,128)}, u32[]{:S(2)}, u32[]{:S(2)}) collective-permute-start(f32[2,2,128,128]{3,2,1,0:T(8,128)S(1)} %slice.144), channel_id=1, source_target_pairs={{1,0},{3,1},{0,2},{2,3},{5,4},{7,5},{4,6},{6,7},{9,8},{11,9},{8,10... | collective-permute-start | bytes 786440 | tf_op jit(solution)/shard_map/ppermute | solution.py:333
  10.4 25.5 %collective-permute-start.13 = (f32[2,2,128,128]{3,2,1,0:T(8,128)S(1)}, f32[2,2,128,128]{3,2,1,0:T(8,128)S(1)}, u32[]{:S(2)}, u32[]{:S(2)}) collective-permute-start(f32[2,2,128,128]{3,2,1,0:T(8,128)S(1)} %get-tuple-element.154), channel_id=1, source_target_pairs={{28,0},{29,1},{30,2},{31,3},{0,4},{1,5},{2,6},{3,7},{4,8},{5,9},{6... | collective-permute-start | bytes 786440 | tf_op jit(solution)/shard_map/ppermute | solution.py:333
  13.1 22.8 %collective-permute-start.11 = (f32[2,2,128,128]{3,2,1,0:T(8,128)S(1)}, f32[2,2,128,128]{3,2,1,0:T(8,128)S(1)}, u32[]{:S(2)}, u32[]{:S(2)}) collective-permute-start(f32[2,2,128,128]{3,2,1,0:T(8,128)S(1)} %get-tuple-element.155), channel_id=1, source_target_pairs={{4,0},{5,1},{6,2},{7,3},{8,4},{9,5},{10,6},{11,7},{12,8},{13,9},{1... | collective-permute-start | bytes 786440 | tf_op jit(solution)/shard_map/ppermute | solution.py:333
  20.6 1.9 %copy-start = (f32[1,1,2,2,6,2,128,128]{7,6,5,4,3,2,1,0:T(8,128)S(1)}, f32[1,1,2,2,6,2,128,128]{7,6,5,4,3,2,1,0:T(8,128)}, u32[]{:S(2)}) copy-start(f32[1,1,2,2,6,2,128,128]{7,6,5,4,3,2,1,0:T(8,128)} %param.9) | copy-start | bytes 9437188
  22.5 5.0 %copy-start.7 = (f32[3,3]{1,0:T(4,128)S(1)}, f32[3,3]{1,0:T(4,128)}, u32[]{:S(2)}) copy-start(f32[3,3]{1,0:T(4,128)} %param.13) | copy-start | bytes 112
  22.5 6.1 %copy-start.8 = (s32[10,4]{0,1:T(4,128)S(1)}, s32[10,4]{0,1:T(4,128)}, u32[]{:S(2)}) copy-start(s32[10,4]{0,1:T(4,128)} %constant.31.clone) | copy-start | bytes 484
  22.5 6.3 %copy-start.9 = (f32[6]{0:T(128)S(1)}, f32[6]{0:T(128)}, u32[]{:S(2)}) copy-start(f32[6]{0:T(128)} %param.12) | copy-start | bytes 76
  27.6 24.2 %copy-start.2 = (f32[1,1,2,2,2,128,128]{6,5,4,3,2,1,0:T(8,128)S(1)}, f32[1,1,2,2,2,128,128]{6,5,4,3,2,1,0:T(8,128)}, u32[]{:S(2)}) copy-start(f32[1,1,2,2,2,128,128]{6,5,4,3,2,1,0:T(8,128)} %param.10) | copy-start | bytes 1572868
  35.9 11.6 %collective-permute-start.14 = (f32[4,2,128,128]{3,2,1,0:T(8,128)S(1)}, f32[4,2,128,128]{3,2,1,0:T(8,128)}, u32[]{:S(2)}, u32[]{:S(2)}) collective-permute-start(f32[4,2,128,128]{3,2,1,0:T(8,128)S(1)} %pad_maximum_fusion.4), channel_id=1, source_target_pairs={{32,0},{33,1},{34,2},{35,3},{36,4},{37,5},{38,6},{39,7},{40,8},{41... | collective-permute-start | bytes 1572872 | tf_op jit(solution)/shard_map/ppermute | solution.py:333
  36.1 18.9 %collective-permute-start.15 = (f32[3,2,128,128]{3,2,1,0:T(8,128)S(1)}, f32[3,2,128,128]{3,2,1,0:T(8,128)}, u32[]{:S(2)}, u32[]{:S(2)}) collective-permute-start(f32[3,2,128,128]{3,2,1,0:T(8,128)S(1)} %pad_maximum_fusion.5), channel_id=1, source_target_pairs={{1,0},{3,1},{0,2},{2,3},{5,4},{7,5},{4,6},{6,7},{9,8},{11,9},{8,10... | collective-permute-start | bytes 1179656 | tf_op jit(solution)/shard_map/ppermute | solution.py:333
  38.3 16.8 %collective-permute-start.17 = (f32[3,2,128,128]{3,2,1,0:T(8,128)S(1)}, f32[3,2,128,128]{3,2,1,0:T(8,128)S(1)}, u32[]{:S(2)}, u32[]{:S(2)}) collective-permute-start(f32[3,2,128,128]{3,2,1,0:T(8,128)S(1)} %pad_maximum_fusion.6), channel_id=1, source_target_pairs={{2,0},{0,1},{3,2},{1,3},{6,4},{4,5},{7,6},{5,7},{10,8},{8,9},{11,1... | collective-permute-start | bytes 1179656 | tf_op jit(solution)/shard_map/ppermute | solution.py:333
  48.6 6.4 %collective-permute-start.19 = (f32[2,2,128,128]{3,2,1,0:T(8,128)S(1)}, f32[2,2,128,128]{3,2,1,0:T(8,128)}, u32[]{:S(2)}, u32[]{:S(2)}) collective-permute-start(f32[2,2,128,128]{3,2,1,0:T(8,128)S(1)} %get-tuple-element.150), channel_id=1, source_target_pairs={{2,0},{0,1},{3,2},{1,3},{6,4},{4,5},{7,6},{5,7},{10,8},{8,9},{11,1... | collective-permute-start | bytes 786440 | tf_op jit(solution)/shard_map/ppermute | solution.py:333
  49.4 8.0 %collective-permute-start.18 = (f32[2,2,128,128]{3,2,1,0:T(8,128)S(1)}, f32[2,2,128,128]{3,2,1,0:T(8,128)}, u32[]{:S(2)}, u32[]{:S(2)}) collective-permute-start(f32[2,2,128,128]{3,2,1,0:T(8,128)S(1)} %get-tuple-element.151), channel_id=1, source_target_pairs={{1,0},{3,1},{0,2},{2,3},{5,4},{7,5},{4,6},{6,7},{9,8},{11,9},{8,10... | collective-permute-start | bytes 786440 | tf_op jit(solution)/shard_map/ppermute | solution.py:333
  92.9 3.8 %collective-permute-start.23 = (f32[2,128,128]{2,1,0:T(8,128)S(1)}, f32[2,128,128]{2,1,0:T(8,128)S(1)}, u32[]{:S(2)}, u32[]{:S(2)}) collective-permute-start(f32[2,128,128]{2,1,0:T(8,128)S(1)} %get-tuple-element.124), channel_id=1, source_target_pairs={{0,1},{1,3},{2,0},{3,2},{4,5},{5,7},{6,4},{7,6},{8,9},{9,11},{10,8... | collective-permute-start | bytes 393224 | tf_op jit(solution)/shard_map/ppermute | solution.py:338
  93.3 5.0 %collective-permute-start.24 = (f32[2,128,128]{2,1,0:T(8,128)S(1)}, f32[2,128,128]{2,1,0:T(8,128)S(1)}, u32[]{:S(2)}, u32[]{:S(2)}) collective-permute-start(f32[2,128,128]{2,1,0:T(8,128)S(1)} %get-tuple-element.125), channel_id=1, source_target_pairs={{0,2},{1,0},{2,3},{3,1},{4,6},{5,4},{6,7},{7,5},{8,10},{9,8},{10,1... | collective-permute-start | bytes 393224 | tf_op jit(solution)/shard_map/ppermute | solution.py:338
  93.5 10.3 %collective-permute-start.21 = (f32[4,128,128]{2,1,0:T(8,128)S(1)}, f32[4,128,128]{2,1,0:T(8,128)S(1)}, u32[]{:S(2)}, u32[]{:S(2)}) collective-permute-start(f32[4,128,128]{2,1,0:T(8,128)S(1)} %get-tuple-element.121), channel_id=1, source_target_pairs={{0,2},{1,0},{2,3},{3,1},{4,6},{5,4},{6,7},{7,5},{8,10},{9,8},{10,1... | collective-permute-start | bytes 786440 | tf_op jit(solution)/shard_map/ppermute | solution.py:338
  95.4 8.4 %collective-permute-start.20 = (f32[5,128,128]{2,1,0:T(8,128)S(1)}, f32[5,128,128]{2,1,0:T(8,128)S(1)}, u32[]{:S(2)}, u32[]{:S(2)}) collective-permute-start(f32[5,128,128]{2,1,0:T(8,128)S(1)} %get-tuple-element.120), channel_id=1, source_target_pairs={{0,1},{1,3},{2,0},{3,2},{4,5},{5,7},{6,4},{7,6},{8,9},{9,11},{10,8... | collective-permute-start | bytes 983048 | tf_op jit(solution)/shard_map/ppermute | solution.py:338
  98.3 8.5 %collective-permute-start.25 = (f32[4,128,128]{2,1,0:T(8,128)S(1)}, f32[4,128,128]{2,1,0:T(8,128)S(1)}, u32[]{:S(2)}, u32[]{:S(2)}) collective-permute-start(f32[4,128,128]{2,1,0:T(8,128)S(1)} %maximum_add_fusion.1), channel_id=1, source_target_pairs={{0,32},{1,33},{2,34},{3,35},{4,36},{5,37},{6,38},{7,39},{8,40},{9,... | collective-permute-start | bytes 786440 | tf_op jit(solution)/shard_map/ppermute | solution.py:338
  103.9 16.0 %collective-permute-start.22 = (f32[4,128,128]{2,1,0:T(8,128)S(1)}, f32[4,128,128]{2,1,0:T(8,128)S(1)}, u32[]{:S(2)}, u32[]{:S(2)}) collective-permute-start(f32[4,128,128]{2,1,0:T(8,128)S(1)} %maximum_add_fusion), channel_id=1, source_target_pairs={{0,32},{1,33},{2,34},{3,35},{4,36},{5,37},{6,38},{7,39},{8,40},{9,... | collective-permute-start | bytes 786440 | tf_op jit(solution)/shard_map/ppermute | solution.py:338
  106.8 8.7 %collective-permute-start.27 = (f32[2,128,128]{2,1,0:T(8,128)S(1)}, f32[2,128,128]{2,1,0:T(8,128)S(1)}, u32[]{:S(2)}, u32[]{:S(2)}) collective-permute-start(f32[2,128,128]{2,1,0:T(8,128)S(1)} %get-tuple-element.159), channel_id=1, source_target_pairs={{0,28},{1,29},{2,30},{3,31},{4,0},{5,1},{6,2},{7,3},{8,4},{9,5},{1... | collective-permute-start | bytes 393224 | tf_op jit(solution)/shard_map/ppermute | solution.py:338
  111.1 8.9 %collective-permute-start.26 = (f32[2,128,128]{2,1,0:T(8,128)S(1)}, f32[2,128,128]{2,1,0:T(8,128)S(1)}, u32[]{:S(2)}, u32[]{:S(2)}) collective-permute-start(f32[2,128,128]{2,1,0:T(8,128)S(1)} %get-tuple-element.160), channel_id=1, source_target_pairs={{0,4},{1,5},{2,6},{3,7},{4,8},{5,9},{6,10},{7,11},{8,12},{9,13},{1... | collective-permute-start | bytes 393224 | tf_op jit(solution)/shard_map/ppermute | solution.py:338
where the time goes:
time: 123 us; the launch traced here: 122 us
  waiting for transfers between devices  33 us (27%)
  starting transfers between devices  27.6 us (22%)
  blocking collectives  27.1 us (22%)
  Pallas kernels  17.6 us (14%)
  local copies, waits for them, and re-layouts  6.95 us (6%)
  other arithmetic  5.85 us (5%)
  between operations  3.94 us (3%)
    ppermute x10, starting transfers between devices, fetch(): return lax.ppermute(jnp.concatenate(blocks, 0), AXES, route)  19.1 us
    all_to_all x1, blocking collectives, over_all(): lax.all_to_all(jnp.broadcast_to(x[None], (NYZ,) + x.shape), 'kyz', 0, 0)  18.9 us
    ppermute x10, waiting for transfers between devices, fetch(): return lax.ppermute(jnp.concatenate(blocks, 0), AXES, route)  17.7 us
    ppermute x8, waiting for transfers between devices, give_back(): return lax.ppermute(block, AXES, route)  15.3 us
    ppermute x8, starting transfers between devices, give_back(): return lax.ppermute(block, AXES, route)  8.46 us
    pallas_call x2, Pallas kernels, product_call(): pl.pallas_call(kernel, in_specs=[SMEM] * len(tables) + [VMEM] * len(array...  8.29 us
    all_to_all x1, blocking collectives, over_all(): x = jnp.sum(lax.all_to_all(copies, 'kx', 0, 0), 0)  8.24 us
    pallas_call x1, Pallas kernels, left_products(): pl.pallas_call(left_kernel, grid=(4,), in_specs=[pl.BlockSpec((1, 2, J, J...  5.03 us
  transfers between devices with their start and end apart: 18, of which 8 were waited for; matrix products, arithmetic and copies ran while one was open for 9% of the time, Pallas kernels for 7%

commit v1 on v0

--- a/solution.py
+++ b/solution.py
@@ -2,7 +2,6 @@
 
 import jax
 import jax.numpy as jnp
-import numpy as np
 from jax import lax
 from jax.experimental import pallas as pl
 from jax.experimental.pallas import tpu as pltpu
@@ -39,13 +38,13 @@
     [((0, 1, 1), 0), ((1, 0, 1), 0), ((1, 0, 1), 2)],
     [((0, 0, -1), 3)],
     [((0, 1, -1), 1), ((1, 0, -1), 1), ((1, 0, -1), 3)],
-    [((1, 1, 1), 0), ((1, -1, 1), 2)],
-    [((1, 1, -1), 1), ((1, -1, -1), 3)],
+    [((0, 0, -1), 3), ((0, 0, -1), 1)],
+    [((0, 0, 1), 2), ((0, 0, 1), 0)],
 )
 SIZES = [len(group) for group in GROUPS]
 SLOTS = sum(SIZES)
-BACK = SIZES[:4] + [SIZES[4] + SIZES[5], SIZES[6] + SIZES[7]] + SIZES[8:]
-SLOT_OF = {where: i for i, where in enumerate(sum(GROUPS, []))}
+CORNER = SLOTS - 4
+SLOT_OF = {where: i for i, where in enumerate(sum(GROUPS, [])[:CORNER])}
 
 
 def place(step, k):
@@ -61,13 +60,23 @@
     return x * NYZ + y * 4 + GRAY[g]
 
 
-def upper_slots(step):
-    return [SLOT_OF[place(step, k)] for k in range(4)]
-
-
-UNIT_SLOTS = [upper_slots(step) for step in UNITS]
-TABLE = np.array([upper_slots(step) for step in DIAGONALS], np.int32)
-CODES = np.array([(s[0] + 1) * 9 + (s[1] + 1) * 3 + s[2] + 1 for s in UNITS + DIAGONALS], np.int32)
+def pair_slots(step, corner):
+    lower, upper = [], []
+    for k in range(4):
+        (dx, dy, dz), t = place(step, k)
+        if dx and dy and dz:
+            lower.append(CORNER + corner)
+            upper.append(SLOT_OF[((dx, dy, 0), t)])
+        else:
+            lower.append(k)
+            upper.append(SLOT_OF[((dx, dy, dz), t)])
+    return lower, upper
+
+
+CORNERS = [(1, 1, 1), (1, -1, 1), (1, 1, -1), (1, -1, -1)]
+UNIT_SLOTS = [pair_slots(step, 0)[1] for step in UNITS]
+TABLE = [pair_slots(step, CORNERS.index(step) if step in CORNERS else 0) for step in DIAGONALS]
+CODES = [(s[0] + 1) * 9 + (s[1] + 1) * 3 + s[2] + 1 for s in UNITS + DIAGONALS]
 
 
 def halves(x):
@@ -103,33 +112,98 @@
         ref[at, J:, J:] = part_re if sign > 0 else -part_re
 
 
-def left_kernel(u_ref, m_ref, v_ref, b_hi, b_lo):
+def plan_kernel(offsets, weights, basis, rows, corner_rows, ends, row_data, flipped):
+    codes = [(offsets[r, 0] + 1) * 9 + (offsets[r, 1] + 1) * 3 + offsets[r, 2] + 1 for r in range(NB)]
+    for j in range(NB):
+        rows[j] = 0
+    for i in range(3):
+        for k in range(4):
+            ends[0, i, k] = k
+            ends[1, i, k] = k
+    count, any_flip = 0, 0
+    for i, code in enumerate(CODES):
+        row, found, flip = 0, 0, 0
+        for r in range(NB):
+            along, against = codes[r] == code, codes[r] == 26 - code
+            row += jnp.where(along | against, r, 0)
+            found += jnp.where(along | against, 1, 0)
+            flip += jnp.where(against, 1, 0)
+        if i < 3:
+            rows[i] = row
+            continue
+        if DIAGONALS[i - 3] in CORNERS:
+            corner_rows[CORNERS.index(DIAGONALS[i - 3])] = row
+        place_at = jnp.minimum(count, 2)
+
+        @pl.when(found > 0)
+        def _():
+            rows[3 + place_at] = row
+            lower, upper = TABLE[i - 3]
+            for k in range(4):
+                ends[0, place_at, k] = jnp.where(flip > 0, upper[k], lower[k])
+                ends[1, place_at, k] = jnp.where(flip > 0, lower[k], upper[k])
+
+        count += found
+        any_flip += flip
+    flipped[0] = any_flip
+    for j in range(NB):
+        row = rows[j]
+        row_data[j, 0] = weights[row]
+        for c in range(3):
+            step = offsets[row, 0].astype(jnp.float32) * basis[0, c]
+            for x in range(1, 3):
+                step += offsets[row, x].astype(jnp.float32) * basis[x, c]
+            row_data[j, 1 + c] = step
+
+
+def make_rows(offsets, weights, basis):
+    whole = jnp.int32, jnp.float32
+    shapes = [((NB,), 0), ((4,), 0), ((2, 3, 4), 0), ((NB, 4), 1), ((1,), 0)]
+    return pl.pallas_call(
+        plan_kernel,
+        in_specs=[SMEM] * 3,
+        out_specs=[SMEM] * len(shapes),
+        out_shape=[jax.ShapeDtypeStruct(shape, whole[kind]) for shape, kind in shapes],
+        name="make_rows",
+    )(offsets, weights, basis)
+
+
+def left_kernel(corner_rows, u_ref, m_ref, v_ref, corner_ref, b_hi, b_lo):
     a_hi, a_lo = halves(jnp.concatenate([u_ref[0, 0].T, u_ref[0, 1].T], 1))
     for j in range(NB):
         block(b_hi, b_lo, j % 2, m_ref[0, j, 0], m_ref[0, j, 1], -1)
         made = three(a_hi, a_lo, b_hi[j % 2], b_lo[j % 2])
         v_ref[0, j, 0] = made[:, :J]
         v_ref[0, j, 1] = made[:, J:]
-
-
-def left_products(own_u, local_m):
+    corner_ref[0] = v_ref[0, corner_rows[corner_of(pl.program_id(0))]]
+
+
+def corner_of(k):
+    return jnp.where(k == 3, 0, jnp.where(k == 1, 1, jnp.where(k == 2, 2, 3)))
+
+
+def left_products(corner_rows, own_u, local_m):
     return pl.pallas_call(
         left_kernel,
         grid=(4,),
         in_specs=[
+            SMEM,
             pl.BlockSpec((1, 2, J, J), lambda k: (k, 0, 0, 0)),
             pl.BlockSpec((1, NB, 2, J, J), lambda k: (k, 0, 0, 0, 0)),
         ],
-        out_specs=pl.BlockSpec((1, NB, 2, J, J), lambda k: (k, 0, 0, 0, 0)),
+        out_specs=[
+            pl.BlockSpec((1, NB, 2, J, J), lambda k: (k, 0, 0, 0, 0)),
+            pl.BlockSpec((1, 2, J, J), lambda k: (corner_of(k), 0, 0, 0)),
+        ],
         scratch_shapes=[
             pltpu.VMEM((2, 2 * J, 2 * J), jnp.bfloat16),
             pltpu.VMEM((2, 2 * J, 2 * J), jnp.bfloat16),
         ],
-        out_shape=jax.ShapeDtypeStruct((4, NB, 2, J, J), jnp.float32),
+        out_shape=[jax.ShapeDtypeStruct((4, NB, 2, J, J), jnp.float32), mats(4)],
         compiler_params=PARAMS,
         cost_estimate=pl.CostEstimate(flops=1 << 32, bytes_accessed=8 << 20, transcendentals=0),
         name="left_products",
-    )(own_u, local_m)
+    )(corner_rows, own_u, local_m)
 
 
 def write_pair(p_ref, d_ref, at, left_re, left_im, right_re, right_im, b_hi, b_lo):
@@ -172,14 +246,15 @@
 
 
 def diagonal_kernel(ends, rows, row_data, so_far_ref, *refs, any_sign):
-    parts, rest = refs[: len(SIZES)], refs[len(SIZES) :]
+    sizes = SIZES if any_sign else SIZES[:-2]
+    parts, rest = refs[: len(sizes)], refs[len(sizes) :]
     if any_sign:
         v_ref, far_ref, *rest = rest
     else:
-        v_ref, *rest = rest
+        v_ref, corner_ref, *rest = rest
     p_ref, d_ref, phase_ref, sum_ref, slots, b_hi, b_lo = rest
     at = 0
-    for ref, n in zip(parts, SIZES):
+    for ref, n in zip(parts, sizes):
         slots[at : at + n] = ref[...]
         at += n
     for p in range(12):
@@ -188,8 +263,10 @@
         if any_sign:
             left_re, left_im = far_ref[low, j, 0], far_ref[low, j, 1]
         else:
-            row = rows[3 + j]
-            left_re, left_im = v_ref[k, row, 0], v_ref[k, row, 1]
+            row, here = rows[3 + j], low < 4
+            own, got = jnp.minimum(low, 3), jnp.maximum(low - CORNER, 0)
+            left_re = jnp.where(here, v_ref[own, row, 0], corner_ref[got, 0])
+            left_im = jnp.where(here, v_ref[own, row, 1], corner_ref[got, 1])
         write_pair(p_ref, d_ref, p, left_re, left_im, slots[up, 0], slots[up, 1], b_hi, b_lo)
     total = write_phases(row_data, 3, d_ref, phase_ref, [so_far_ref[i : i + 1] for i in range(4)])
     for i in range(NKX):
@@ -217,12 +294,12 @@
     return product_call(unit_kernel, "unit_products", [rows, row_data], [own, x, y, z, v], (4,))
 
 
-def diagonal_products(ends, rows, row_data, so_far, parts, v, far=None):
+def diagonal_products(ends, rows, row_data, so_far, parts, v, corner_v, far=None):
     return product_call(
         functools.partial(diagonal_kernel, any_sign=far is not None),
         "diagonal_products",
         [ends, rows, row_data],
-        [so_far, *parts, v] + ([] if far is None else [far]),
+        [so_far, *parts, v] + ([corner_v] if far is None else [far]),
         (NKX, 4),
         [pltpu.VMEM((SLOTS, 2, J, J), jnp.float32)],
     )
@@ -233,8 +310,8 @@
 
 
 def term_kernel(ends, row_data, pu_ref, du_ref, phu_ref, pd_ref, dd_ref, phd_ref, got_ref, *refs):
-    total_ref, outs = refs[0], refs[1 : 1 + len(BACK)]
-    plain, cross, rows_a, rows_b, turned_a, turned_b = refs[1 + len(BACK) :]
+    total_ref, outs = refs[0], refs[1 : 1 + len(SIZES)]
+    plain, cross, rows_a, rows_b, turned_a, turned_b = refs[1 + len(SIZES) :]
     total = jnp.sum(got_ref[...], 0)
     total_ref[...] = total
     centres = (-2.0 / NK) * total[:3]
@@ -285,7 +362,7 @@
             plain[up, part, :] -= one
             cross[up, part, :] -= two
     at = 0
-    for ref, n in zip(outs, BACK):
+    for ref, n in zip(outs, SIZES):
         for i in range(n):
             ref[i] = 2.0 * (plain[at] + cross[at].T)
             at += 1
@@ -295,8 +372,8 @@
     return pl.pallas_call(
         term_kernel,
         in_specs=[SMEM, SMEM] + [VMEM] * 7,
-        out_specs=[VMEM] * (1 + len(BACK)),
-        out_shape=[jax.ShapeDtypeStruct((4, J), jnp.float32)] + [reals(n) for n in BACK],
+        out_specs=[VMEM] * (1 + len(SIZES)),
+        out_shape=[jax.ShapeDtypeStruct((4, J), jnp.float32)] + [reals(n) for n in SIZES],
         scratch_shapes=[pltpu.VMEM((SLOTS, J, J), jnp.float32)] * 2 + [pltpu.VMEM((J, J), jnp.float32)] * 4,
         compiler_params=PARAMS,
         cost_estimate=pl.CostEstimate(flops=1 << 24, bytes_accessed=8 << 20, transcendentals=0),
@@ -308,10 +385,14 @@
     for k in range(4):
         total = own_ref[k] + x_ref[k]
         total += y_ref[k] if k < 2 else y_back_ref[k - 2]
-        if k % 2 == 0:
-            total += z_ref[k // 2]
-        if k == 3:
-            total += z_back_ref[0]
+        if k == 0:
+            total += z_ref[0] + z_ref[3]
+        elif k == 1:
+            total += z_back_ref[2]
+        elif k == 2:
+            total += z_ref[1] + z_ref[2]
+        else:
+            total += z_back_ref[0] + z_back_ref[1]
         turned = total.T
         g_ref[k, 0] = 0.5 * (total - turned)
         g_ref[k, 1] = 0.5 * (total + turned)
@@ -350,65 +431,62 @@
     xy = fetch(X, y, y_back)
     beside = fetch(Z, y[0:1], x[0::2])
     beside_back = fetch(Z_BACK, y[1:2], x[1::2])
-    corner = fetch(Z, xy[0::2])
-    corner_back = fetch(Z_BACK, xy[1::2])
-    return own, x, y, xy, z, beside, z_back, beside_back, corner, corner_back
-
-
-def fold_halo(own, x, y, xy, z, z_back, corner, corner_back):
-    corner = give_back(Z, corner)
-    corner_back = give_back(Z_BACK, corner_back)
-    z = give_back(Z, z)
-    z_back = give_back(Z_BACK, z_back)
-    corners = [corner[0:1], corner_back[0:1], corner[1:2], corner_back[1:2]]
-    xy = give_back(X, xy + jnp.concatenate(corners, 0))
-    sides = [z[3:4], z_back[2:3], z[4:5], z_back[3:4]]
+    return own, x, y, xy, z, beside, z_back, beside_back
+
+
+def corners(field):
+    return fetch(Z_BACK, field[0:2]), fetch(Z, field[2:4])
+
+
+def fold_halo(own, x, y, xy, z, beside, z_back, beside_back, corner, corner_back):
+    xy = give_back(X, xy)
+    beside = give_back(Z, beside)
+    beside_back = give_back(Z_BACK, beside_back)
+    sides = [beside[1:2], beside_back[1:2], beside[2:3], beside_back[2:3]]
     x = give_back(X, x + jnp.concatenate(sides, 0))
-    y = give_back(Y, y + xy[0:2] + jnp.concatenate([z[2:3], z_back[1:2]], 0))
+    beside, z, corner_back, z_back, corner = lax.optimization_barrier(
+        (beside, z, corner_back, z_back, corner)
+    )
+    z = give_back(Z, jnp.concatenate([z, corner_back], 0))
+    z_back = give_back(Z_BACK, jnp.concatenate([z_back, corner], 0))
+    y = give_back(Y, y + xy[0:2] + jnp.concatenate([beside[0:1], beside_back[0:1]], 0))
     y_back = give_back(Y_BACK, xy[2:4])
     return fold_terms(own, x, y, y_back, z, z_back)
 
 
 def over_all(copies):
-    x = jnp.sum(lax.all_to_all(copies, "kx", 0, 0), 0)
-    return lax.all_to_all(jnp.broadcast_to(x[None], (NYZ,) + x.shape), "kyz", 0, 0)
+    x = copies[0] + lax.ppermute(copies[0], "kyz", [(i, i ^ 1) for i in range(NYZ)])
+    one_core = [[core + 2 * i for i in range(NYZ // 2)] for core in range(2)]
+    copies = jnp.broadcast_to(x[None], (NYZ // 2,) + x.shape)
+    x = jnp.sum(lax.all_to_all(copies, "kyz", 0, 0, axis_index_groups=one_core), 0)
+    copies = jnp.broadcast_to(x[None], (NKX,) + x.shape)
+    return lax.all_to_all(copies, "kx", 0, 0)
 
 
 def on_device(intersections, rotations, offsets, weights, basis):
     own_u = rotations.reshape(4, 2, J, J)
     local_m = intersections.reshape(4, NB, 2, J, J)
     parts = halo(own_u)
-    v = left_products(own_u, local_m)
-
-    code = (offsets[:, 0] + 1) * 9 + (offsets[:, 1] + 1) * 3 + offsets[:, 2] + 1
-    with_sign = jnp.asarray(CODES)[:, None] == code[None, :]
-    against = 26 - jnp.asarray(CODES)[:, None] == code[None, :]
-    here = with_sign | against
-    rank = jnp.cumsum(jnp.any(here[3:], 1).astype(jnp.int32))
-    nth = (rank[None] == jnp.arange(1, 4, dtype=jnp.int32)[:, None])[:, :, None] & here[None, 3:]
-    chosen = jnp.concatenate([here[:3], jnp.any(nth, 1)], 0)
-    rows = jnp.sum(jnp.where(chosen, jnp.arange(NB, dtype=jnp.int32)[None], 0), 1)
-    upper = jnp.sum(jnp.where(jnp.any(nth, 2)[:, :, None], jnp.asarray(TABLE), 0), 1)
-    lower = jnp.broadcast_to(jnp.arange(4, dtype=jnp.int32)[None], (3, 4))
-    flipped = jnp.any(nth & against[None, 3:], (1, 2))
-    ends = jnp.stack(
-        [jnp.where(flipped[:, None], upper, lower), jnp.where(flipped[:, None], lower, upper)]
-    )
-    step_vec = jnp.sum(offsets.astype(jnp.float32)[:, :, None] * basis[None], 1)
-    row_data = jnp.concatenate([weights[:, None], step_vec], 1)
-    row_data = jnp.sum(jnp.where(chosen[:, :, None], row_data[None], 0.0), 1)
-
+    rows, corner_rows, ends, row_data, flipped = make_rows(offsets, weights, basis)
+    v, corner_v = left_products(corner_rows, own_u, local_m)
     *unit, so_far = unit_products(rows, row_data, own_u, parts[1], parts[2], parts[4], v)
 
-    def usual(ends, rows, row_data, so_far, v, *parts):
-        return diagonal_products(ends, rows, row_data, so_far, parts, v)
-
-    def any_sign(ends, rows, row_data, so_far, v, *parts):
-        far = halo(jnp.stack([v[:, rows[j]] for j in range(3, NB)], 1))
-        return diagonal_products(ends, rows, row_data, so_far, parts, v, jnp.concatenate(far, 0))
+    corner_v, _ = lax.optimization_barrier((corner_v, parts[1]))
+    corner_v = jnp.concatenate(corners(corner_v), 0)
+
+    def usual(ends, rows, row_data, so_far, v, corner_v, *parts):
+        return diagonal_products(ends, rows, row_data, so_far, parts, v, corner_v)
+
+    def any_sign(ends, rows, row_data, so_far, v, corner_v, *parts):
+        own_v = jnp.stack([v[:, rows[j]] for j in range(3, NB)], 1)
+        own = jnp.concatenate([parts[0][:, None], own_v], 1)
+        low = corners(jnp.concatenate([own[3:4], own[1:3], own[0:1]], 0))
+        far = jnp.concatenate(halo(own_v) + tuple(block[:, 1:] for block in low), 0)
+        parts += tuple(block[:, 0] for block in low)
+        return diagonal_products(ends, rows, row_data, so_far, parts, v, corner_v, far)
 
     *diagonal, part = lax.cond(
-        jnp.any(flipped), any_sign, usual, ends, rows, row_data, so_far, v, *parts
+        flipped[0] > 0, any_sign, usual, ends, rows, row_data, so_far, v, corner_v, *parts
     )
     got = over_all(part)
     total, *terms = pair_terms(ends, row_data, unit, diagonal, got)

time: 123 us -> 112 us (0.911)
  waiting for transfers between devices: 33 us -> 17.1 us
  starting transfers between devices: 27.6 us -> 37.7 us
  blocking collectives: 27.1 us -> 22.1 us
  other arithmetic: 5.85 us -> 2.03 us
  Pallas kernels: 17.6 us -> 19.7 us
  local copies, waits for them, and re-layouts: 6.95 us -> 8.55 us
    ppermute x10, waiting for transfers between devices: 17.7 us -> 8.83 us  [fetch(): return lax.ppermute(jnp.concatenate(blocks, 0), AXES, route)]
    ppermute x8, waiting for transfers between devices: 15.3 us -> 7.45 us  [give_back(): return lax.ppermute(block, AXES, route)]
    all_to_all x2, blocking collectives: 27.1 us -> 22.1 us  [the longest x1 14.7 us: over_all(): lax.all_to_all(copies, 'kyz', 0, 0, axis_index_groups=one_core)]
    ppermute x10, starting transfers between devices: 19.1 us -> 23.6 us  [fetch(): return lax.ppermute(jnp.concatenate(blocks, 0), AXES, route)]
    ppermute x8, starting transfers between devices: 8.46 us -> 12.2 us  [give_back(): return lax.ppermute(block, AXES, route)]
    pallas_call x1 -> x2, Pallas kernels: 5.03 us -> 7.04 us  [the longest x1 5.13 us: left_products(): pl.pallas_call(left_kernel, grid=(4,), in_specs=[SMEM, pl.BlockSpec((1, 2...]
    unnamed x10 -> x9, local copies, waits for them, and re-layouts: 1.91 us -> 3.9 us
    ppermute x0 -> x1, starting transfers between devices: none -> 1.97 us  [over_all(): lax.ppermute(copies[0], 'kyz', [(i, i ^ 1) for i in range(NYZ)])]
  transfers between devices with their start and end apart: 18 -> 19, of which waited for: 8 -> 7; matrix products, arithmetic and copies ran while one was open for 9% -> 7% of each run, Pallas kernels for 7% -> 9%
where the time goes in v1:
time: 112 us; the launch traced here: 111 us
  starting transfers between devices  37.7 us (34%)
  blocking collectives  22.1 us (20%)
  Pallas kernels  19.7 us (18%)
  waiting for transfers between devices  17.1 us (15%)
  local copies, waits for them, and re-layouts  8.55 us (8%)
  between operations  4 us (4%)
  other arithmetic  2.03 us (2%)
    ppermute x10, starting transfers between devices, fetch(): return lax.ppermute(jnp.concatenate(blocks, 0), AXES, route)  23.6 us
    all_to_all x1, blocking collectives, over_all(): lax.all_to_all(copies, 'kyz', 0, 0, axis_index_groups=one_core)  14.7 us
    ppermute x8, starting transfers between devices, give_back(): return lax.ppermute(block, AXES, route)  12.2 us
    ppermute x10, waiting for transfers between devices, fetch(): return lax.ppermute(jnp.concatenate(blocks, 0), AXES, route)  8.83 us
    pallas_call x2, Pallas kernels, product_call(): pl.pallas_call(kernel, in_specs=[SMEM] * len(tables) + [VMEM] * len(array...  8.35 us
    ppermute x8, waiting for transfers between devices, give_back(): return lax.ppermute(block, AXES, route)  7.45 us
    all_to_all x1, blocking collectives, over_all(): return lax.all_to_all(copies, 'kx', 0, 0)  7.42 us
    pallas_call x1, Pallas kernels, left_products(): pl.pallas_call(left_kernel, grid=(4,), in_specs=[SMEM, pl.BlockSpec((1, 2...  5.13 us
  transfers between devices with their start and end apart: 19, of which 7 were waited for; matrix products, arithmetic and copies ran while one was open for 7% of the time, Pallas kernels for 9%

profile of v1, /device:TPU:1, one launch (start us, length us, event | category | flops | bytes accessed | tf_op | source)
XLA Modules:
  0.0 111.4 jit_solution(16287375583370061711)
XLA Ops:
  0.6 4.7 %collective-permute-start.10 = (f32[4,2,128,128]{3,2,1,0:T(8,128)}, f32[4,2,128,128]{3,2,1,0:T(8,128)S(1)}, u32[]{:S(2)}, u32[]{:S(2)}) collective-permute-start(f32[4,2,128,128]{3,2,1,0:T(8,128)} %bitcast.21), channel_id=1, source_target_pairs={{32,0},{33,1},{34,2},{35,3},{36,4},{37,5},{38,6},{39,7},{40,8},{41... | collective-permute-start | bytes 1572872 | tf_op jit(solution)/shard_map/ppermute | solution.py:414
  5.4 1.6 %slice.172 = f32[1,2,128,128]{3,2,1,0:T(8,128)} slice(f32[4,2,128,128]{3,2,1,0:T(8,128)} %bitcast.22), slice={[3:4], [0:2], [0:128], [0:128]} | slice | bytes 262144 | tf_op jit(solution)/shard_map/slice | solution.py:430
  10.4 2.7 %collective-permute-start.13 = (f32[2,2,128,128]{3,2,1,0:T(8,128)S(1)}, f32[2,2,128,128]{3,2,1,0:T(8,128)S(1)}, u32[]{:S(2)}, u32[]{:S(2)}) collective-permute-start(f32[2,2,128,128]{3,2,1,0:T(8,128)S(1)} %get-tuple-element.202), channel_id=1, source_target_pairs={{28,0},{29,1},{30,2},{31,3},{0,4},{1,5},{2,6},{3,7},{4,8},{5,9},{6... | collective-permute-start | bytes 786440 | tf_op jit(solution)/shard_map/ppermute | solution.py:414
  13.1 4.9 %collective-permute-start.11 = (f32[2,2,128,128]{3,2,1,0:T(8,128)S(1)}, f32[2,2,128,128]{3,2,1,0:T(8,128)S(1)}, u32[]{:S(2)}, u32[]{:S(2)}) collective-permute-start(f32[2,2,128,128]{3,2,1,0:T(8,128)S(1)} %get-tuple-element.203), channel_id=1, source_target_pairs={{4,0},{5,1},{6,2},{7,3},{8,4},{9,5},{10,6},{11,7},{12,8},{13,9},{1... | collective-permute-start | bytes 786440 | tf_op jit(solution)/shard_map/ppermute | solution.py:414
  19.4 1.9 %make_rows.1 = (s32[6]{0:T(128)S(1)}, s32[4]{0:T(128)}, s32[2,3,4]{2,1,0:T(4,128)S(1)}, f32[6,4]{1,0:T(8,128)S(1)}, s32[1]{0:T(128)}) custom-call(s32[6,3]{1,0:T(8,128)} %copy.10.offsets, f32[6]{0:T(128)} %weights.1, f32[3,3]{1,0:T(4,128)} %basis.1), custom_call_target="tpu_custom_call" | custom-call | tf_op jit(solution)/shard_map/make_rows/pallas_call | solution.py:162
  21.3 1.9 %copy-done = f32[1,1,2,2,6,2,128,128]{7,6,5,4,3,2,1,0:T(8,128)S(1)} copy-done((f32[1,1,2,2,6,2,128,128]{7,6,5,4,3,2,1,0:T(8,128)S(1)}, f32[1,1,2,2,6,2,128,128]{7,6,5,4,3,2,1,0:T(8,128)}, u32[]{:S(2)}) %copy-start) | copy-done | bytes 3145752
  23.9 5.1 %left_products.1 = (f32[4,6,2,128,128]{4,3,2,1,0:T(8,128)}, f32[4,2,128,128]{3,2,1,0:T(8,128)S(1)}) custom-call(s32[4]{0:T(128)S(1)} %copy-done.1, f32[4,2,128,128]{3,2,1,0:T(8,128)} %bitcast.24, f32[4,6,2,128,128]{4,3,2,1,0:T(8,128)S(1)} %bitcast.20), custom_call_target="tpu_custom_call" | custom-call | flops 4294967296 | bytes 8388608 | tf_op jit(solution)/shard_map/left_products/pallas_call | solution.py:186
  29.6 6.2 %collective-permute-done.13 = f32[2,2,128,128]{3,2,1,0:T(8,128)S(1)} collective-permute-done((f32[2,2,128,128]{3,2,1,0:T(8,128)S(1)}, f32[2,2,128,128]{3,2,1,0:T(8,128)S(1)}, u32[]{:S(2)}, u32[]{:S(2)}) %collective-permute-start.13) | collective-permute-done | bytes 262176 | tf_op jit(solution)/shard_map/ppermute | solution.py:414
  36.7 1.7 %collective-permute-start.15 = (f32[3,2,128,128]{3,2,1,0:T(8,128)S(1)}, f32[3,2,128,128]{3,2,1,0:T(8,128)}, u32[]{:S(2)}, u32[]{:S(2)}) collective-permute-start(f32[3,2,128,128]{3,2,1,0:T(8,128)S(1)} %pad_maximum_fusion.15), channel_id=1, source_target_pairs={{1,0},{3,1},{0,2},{2,3},{5,4},{7,5},{4,6},{6,7},{9,8},{11,9},{8,10... | collective-permute-start | bytes 1179656 | tf_op jit(solution)/shard_map/ppermute | solution.py:414
  38.5 1.4 %collective-permute-done.18 = f32[2,2,128,128]{3,2,1,0:T(8,128)S(1)} collective-permute-done((f32[2,2,128,128]{3,2,1,0:T(8,128)S(1)}, f32[2,2,128,128]{3,2,1,0:T(8,128)S(1)}, u32[]{:S(2)}, u32[]{:S(2)}) %collective-permute-start.18) | collective-permute-done | bytes 262176 | tf_op jit(solution)/shard_map/ppermute | solution.py:414
  39.9 7.5 %collective-permute-start.19 = (f32[2,2,128,128]{3,2,1,0:T(8,128)S(1)}, f32[2,2,128,128]{3,2,1,0:T(8,128)S(1)}, u32[]{:S(2)}, u32[]{:S(2)}) collective-permute-start(f32[2,2,128,128]{3,2,1,0:T(8,128)S(1)} %get-tuple-element.199), channel_id=1, source_target_pairs={{1,0},{3,1},{0,2},{2,3},{5,4},{7,5},{4,6},{6,7},{9,8},{11,9},{8,10... | collective-permute-start | bytes 786440 | tf_op jit(solution)/shard_map/ppermute | solution.py:414
  47.4 3.3 %unit_products.1 = (f32[12,2,128,128]{3,2,1,0:T(8,128)S(1)}, f32[2,3,4,128]{3,2,1,0:T(4,128)S(1)}, f32[3,4,128]{2,1,0:T(4,128)S(1)}, f32[4,128]{1,0:T(4,128)S(1)}) custom-call(s32[6]{0:T(128)S(1)} %get-tuple-element.135.rows, f32[6,4]{1,0:T(8,128)S(1)} %get-tuple-element.134.row_data, f32[4,2,128,128]{3,2,1,0:T(8,128)S(1)} %bitcast.25, ...), custom_call_target="tpu_custom_call" | custom-call | flops 4294967296 | bytes 4194304 | tf_op jit(solution)/shard_map/unit_products/pallas_call | solution.py:277
  51.9 5.3 %conditional.1 = ((f32[12,2,128,128]{3,2,1,0:T(8,128)}, f32[2,3,4,128]{3,2,1,0:T(4,128)S(1)}, f32[3,4,128]{2,1,0:T(4,128)S(1)}, f32[8,4,128]{2,1,0:T(4,128)S(1)})) conditional(s32[]{:T(128)} %bitcast.9, (s32[2,3,4]{2,1,0:T(4,128)S(1)}, s32[6]{0:T(128)S(1)}, f32[6,4]{1,0:T(8,128)S(1)}, f32[4,128]{1,0:T(4,128)S(1)}, f32[4,2,128,128]{3,2,1,0:T(8,128)S(1)}, ...), branch_computations={%region_0.0_spmd, %region_1.0_spmd} | conditional | flops 4300406784 | bytes 144704064 | solution.py:488
  52.1 5.1 %diagonal_products.2 = (f32[12,2,128,128]{3,2,1,0:T(8,128)}, f32[2,3,4,128]{3,2,1,0:T(4,128)S(1)}, f32[3,4,128]{2,1,0:T(4,128)S(1)}, f32[8,4,128]{2,1,0:T(4,128)S(1)}) custom-call(s32[2,3,4]{2,1,0:T(4,128)S(1)} %get-tuple-element.70.ends, s32[6]{0:T(128)S(1)} %get-tuple-element.71.rows, f32[6,4]{1,0:T(8,128)S(1)} %get-tuple-element.72.row_data, ...), custom_call_target="tpu_custom_call" | custom-call | flops 4294967296 | bytes 4194304 | tf_op jit(solution)/shard_map/cond/branch_0_fun/diagonal_products/pallas_call | solution.py:277
  57.2 2.0 %collective-permute-start.20 = (f32[4,128]{1,0:T(4,128)S(1)}, f32[4,128]{1,0:T(4,128)S(1)}, u32[]{:S(2)}, u32[]{:S(2)}) collective-permute-start(f32[4,128]{1,0:T(4,128)S(1)} %slice_bitcast_fusion.4), channel_id=1, source_target_pairs={{0,1},{1,0},{2,3},{3,2},{4,5},{5,4},{6,7},{7,6},{8,9},{9,8},{10,11... | collective-permute-start | bytes 6152 | tf_op jit(solution)/shard_map/ppermute | solution.py:458
  60.0 14.7 %all_to_all.10 = f32[16,4,128]{2,1,0:T(4,128)S(1)} all-to-all(f32[16,4,128]{2,1,0:T(4,128)S(1)} %broadcast_in_dim.4), channel_id=1, replica_groups={{0,2,4,6,8,10,12,14,16,18,20,22,24,26,28,30},{1,3,5,7,9,11,13,15,17,19,..., dimensions={0} | all-to-all | bytes 65536 | tf_op jit(solution)/shard_map/all_to_all | solution.py:461
  74.7 7.4 %all_to_all.11.got_ref = f32[8,4,128]{2,1,0:T(4,128)S(1)} all-to-all(f32[8,4,128]{2,1,0:T(4,128)S(1)} %broadcast_in_dim.5), channel_id=1, replica_groups=mesh['kx'=8,'kyz'=32] {'kx'}, dimensions={0} | all-to-all | bytes 32768 | tf_op jit(solution)/shard_map/all_to_all | solution.py:463
  82.1 3.3 %pair_terms.1 = (f32[4,128]{1,0:T(4,128)S(1)}, f32[4,128,128]{2,1,0:T(8,128)S(1)}, f32[4,128,128]{2,1,0:T(8,128)S(1)}, f32[2,128,128]{2,1,0:T(8,128)S(1)}, f32[4...) custom-call(s32[2,3,4]{2,1,0:T(4,128)S(1)} %get-tuple-element.133.en, ...), custom_call_target="tpu_custom_call" | custom-call | flops 16777216 | bytes 8388608 | tf_op jit(solution)/shard_map/pair_terms/pallas_call | solution.py:372
  85.9 2.6 %collective-permute-start.22 = (f32[3,128,128]{2,1,0:T(8,128)S(1)}, f32[3,128,128]{2,1,0:T(8,128)S(1)}, u32[]{:S(2)}, u32[]{:S(2)}) collective-permute-start(f32[3,128,128]{2,1,0:T(8,128)S(1)} %get-tuple-element.152), channel_id=1, source_target_pairs={{0,2},{1,0},{2,3},{3,1},{4,6},{5,4},{6,7},{7,5},{8,10},{9,8},{10,1... | collective-permute-start | bytes 589832 | tf_op jit(solution)/shard_map/ppermute | solution.py:419
  90.1 5.7 %collective-permute-start.28 = (f32[3,128,128]{2,1,0:T(8,128)S(1)}, f32[3,128,128]{2,1,0:T(8,128)S(1)}, u32[]{:S(2)}, u32[]{:S(2)}) collective-permute-start(f32[3,128,128]{2,1,0:T(8,128)S(1)} %pad_maximum_fusion.18), channel_id=1, source_target_pairs={{0,2},{1,0},{2,3},{3,1},{4,6},{5,4},{6,7},{7,5},{8,10},{9,8},{10,1... | collective-permute-start | bytes 589832 | tf_op jit(solution)/shard_map/ppermute | solution.py:419
  97.0 1.9 %collective-permute-start.26 = (f32[2,128,128]{2,1,0:T(8,128)S(1)}, f32[2,128,128]{2,1,0:T(8,128)S(1)}, u32[]{:S(2)}, u32[]{:S(2)}) collective-permute-start(f32[2,128,128]{2,1,0:T(8,128)S(1)} %get-tuple-element.204), channel_id=1, source_target_pairs={{0,28},{1,29},{2,30},{3,31},{4,0},{5,1},{6,2},{7,3},{8,4},{9,5},{1... | collective-permute-start | bytes 393224 | tf_op jit(solution)/shard_map/ppermute | solution.py:419
  101.8 3.9 %collective-permute-done.26.y_back_ref = f32[2,128,128]{2,1,0:T(8,128)S(1)} collective-permute-done((f32[2,128,128]{2,1,0:T(8,128)S(1)}, f32[2,128,128]{2,1,0:T(8,128)S(1)}, u32[]{:S(2)}, u32[]{:S(2)}) %collective-permute-start.26) | collective-permute-done | bytes 131104 | tf_op jit(solution)/shard_map/ppermute | solution.py:419
  105.7 2.0 %collective-permute-done.25.y_ref = f32[2,128,128]{2,1,0:T(8,128)S(1)} collective-permute-done((f32[2,128,128]{2,1,0:T(8,128)S(1)}, f32[2,128,128]{2,1,0:T(8,128)S(1)}, u32[]{:S(2)}, u32[]{:S(2)}) %collective-permute-start.25) | collective-permute-done | bytes 131104 | tf_op jit(solution)/shard_map/ppermute | solution.py:419
  107.7 1.6 %collective-permute-done.23.x_ref = f32[4,128,128]{2,1,0:T(8,128)S(1)} collective-permute-done((f32[4,128,128]{2,1,0:T(8,128)S(1)}, f32[4,128,128]{2,1,0:T(8,128)S(1)}, u32[]{:S(2)}, u32[]{:S(2)}) %collective-permute-start.23) | collective-permute-done | bytes 262176 | tf_op jit(solution)/shard_map/ppermute | solution.py:419
  (56 shorter events, 14.1 us)
Async XLA Ops:
  0.6 35.4 %collective-permute-start.10 = (f32[4,2,128,128]{3,2,1,0:T(8,128)}, f32[4,2,128,128]{3,2,1,0:T(8,128)S(1)}, u32[]{:S(2)}, u32[]{:S(2)}) collective-permute-start(f32[4,2,128,128]{3,2,1,0:T(8,128)} %bitcast.21), channel_id=1, source_target_pairs={{32,0},{33,1},{34,2},{35,3},{36,4},{37,5},{38,6},{39,7},{40,8},{41... | collective-permute-start | bytes 1572872 | tf_op jit(solution)/shard_map/ppermute | solution.py:414
  7.0 44.9 %collective-permute-start.16 = (f32[1,2,128,128]{3,2,1,0:T(8,128)}, f32[1,2,128,128]{3,2,1,0:T(8,128)}, u32[]{:S(2)}, u32[]{:S(2)}) collective-permute-start(f32[1,2,128,128]{3,2,1,0:T(8,128)} %slice.172), channel_id=1, source_target_pairs={{2,0},{0,1},{3,2},{1,3},{6,4},{4,5},{7,6},{5,7},{10,8},{8,9},{11,1... | collective-permute-start | bytes 393224 | tf_op jit(solution)/shard_map/ppermute | solution.py:414
  9.2 29.2 %collective-permute-start.12 = (f32[2,2,128,128]{3,2,1,0:T(8,128)S(1)}, f32[2,2,128,128]{3,2,1,0:T(8,128)}, u32[]{:S(2)}, u32[]{:S(2)}) collective-permute-start(f32[2,2,128,128]{3,2,1,0:T(8,128)S(1)} %slice.137), channel_id=1, source_target_pairs={{1,0},{3,1},{0,2},{2,3},{5,4},{7,5},{4,6},{6,7},{9,8},{11,9},{8,10... | collective-permute-start | bytes 786440 | tf_op jit(solution)/shard_map/ppermute | solution.py:414
  10.4 25.5 %collective-permute-start.13 = (f32[2,2,128,128]{3,2,1,0:T(8,128)S(1)}, f32[2,2,128,128]{3,2,1,0:T(8,128)S(1)}, u32[]{:S(2)}, u32[]{:S(2)}) collective-permute-start(f32[2,2,128,128]{3,2,1,0:T(8,128)S(1)} %get-tuple-element.202), channel_id=1, source_target_pairs={{28,0},{29,1},{30,2},{31,3},{0,4},{1,5},{2,6},{3,7},{4,8},{5,9},{6... | collective-permute-start | bytes 786440 | tf_op jit(solution)/shard_map/ppermute | solution.py:414
  13.1 22.8 %collective-permute-start.11 = (f32[2,2,128,128]{3,2,1,0:T(8,128)S(1)}, f32[2,2,128,128]{3,2,1,0:T(8,128)S(1)}, u32[]{:S(2)}, u32[]{:S(2)}) collective-permute-start(f32[2,2,128,128]{3,2,1,0:T(8,128)S(1)} %get-tuple-element.203), channel_id=1, source_target_pairs={{4,0},{5,1},{6,2},{7,3},{8,4},{9,5},{10,6},{11,7},{12,8},{13,9},{1... | collective-permute-start | bytes 786440 | tf_op jit(solution)/shard_map/ppermute | solution.py:414
  21.3 1.9 %copy-start = (f32[1,1,2,2,6,2,128,128]{7,6,5,4,3,2,1,0:T(8,128)S(1)}, f32[1,1,2,2,6,2,128,128]{7,6,5,4,3,2,1,0:T(8,128)}, u32[]{:S(2)}) copy-start(f32[1,1,2,2,6,2,128,128]{7,6,5,4,3,2,1,0:T(8,128)} %param.7) | copy-start | bytes 9437188
  23.2 0.7 copy-start.1
  35.9 11.5 %copy-start.3 = (f32[1,1,2,2,2,128,128]{6,5,4,3,2,1,0:T(8,128)S(1)}, f32[1,1,2,2,2,128,128]{6,5,4,3,2,1,0:T(8,128)}, u32[]{:S(2)}) copy-start(f32[1,1,2,2,2,128,128]{6,5,4,3,2,1,0:T(8,128)} %param.8) | copy-start | bytes 1572868
  35.9 16.0 %collective-permute-start.14 = (f32[4,2,128,128]{3,2,1,0:T(8,128)S(1)}, f32[4,2,128,128]{3,2,1,0:T(8,128)}, u32[]{:S(2)}, u32[]{:S(2)}) collective-permute-start(f32[4,2,128,128]{3,2,1,0:T(8,128)S(1)} %pad_maximum_fusion.13), channel_id=1, source_target_pairs={{32,0},{33,1},{34,2},{35,3},{36,4},{37,5},{38,6},{39,7},{40,8},{41... | collective-permute-start | bytes 1572872 | tf_op jit(solution)/shard_map/ppermute | solution.py:414
  36.1 3.8 %collective-permute-start.18 = (f32[2,2,128,128]{3,2,1,0:T(8,128)S(1)}, f32[2,2,128,128]{3,2,1,0:T(8,128)S(1)}, u32[]{:S(2)}, u32[]{:S(2)}) collective-permute-start(f32[2,2,128,128]{3,2,1,0:T(8,128)S(1)} %get-tuple-element.198), channel_id=1, source_target_pairs={{2,0},{0,1},{3,2},{1,3},{6,4},{4,5},{7,6},{5,7},{10,8},{8,9},{11,1... | collective-permute-start | bytes 786440 | tf_op jit(solution)/shard_map/ppermute | solution.py:414
  36.7 15.2 %collective-permute-start.15 = (f32[3,2,128,128]{3,2,1,0:T(8,128)S(1)}, f32[3,2,128,128]{3,2,1,0:T(8,128)}, u32[]{:S(2)}, u32[]{:S(2)}) collective-permute-start(f32[3,2,128,128]{3,2,1,0:T(8,128)S(1)} %pad_maximum_fusion.15), channel_id=1, source_target_pairs={{1,0},{3,1},{0,2},{2,3},{5,4},{7,5},{4,6},{6,7},{9,8},{11,9},{8,10... | collective-permute-start | bytes 1179656 | tf_op jit(solution)/shard_map/ppermute | solution.py:414
  38.4 13.5 %collective-permute-start.17 = (f32[3,2,128,128]{3,2,1,0:T(8,128)S(1)}, f32[3,2,128,128]{3,2,1,0:T(8,128)}, u32[]{:S(2)}, u32[]{:S(2)}) collective-permute-start(f32[3,2,128,128]{3,2,1,0:T(8,128)S(1)} %pad_maximum_fusion.16), channel_id=1, source_target_pairs={{2,0},{0,1},{3,2},{1,3},{6,4},{4,5},{7,6},{5,7},{10,8},{8,9},{11,1... | collective-permute-start | bytes 1179656 | tf_op jit(solution)/shard_map/ppermute | solution.py:414
  39.9 11.9 %collective-permute-start.19 = (f32[2,2,128,128]{3,2,1,0:T(8,128)S(1)}, f32[2,2,128,128]{3,2,1,0:T(8,128)S(1)}, u32[]{:S(2)}, u32[]{:S(2)}) collective-permute-start(f32[2,2,128,128]{3,2,1,0:T(8,128)S(1)} %get-tuple-element.199), channel_id=1, source_target_pairs={{1,0},{3,1},{0,2},{2,3},{5,4},{7,5},{4,6},{6,7},{9,8},{11,9},{8,10... | collective-permute-start | bytes 786440 | tf_op jit(solution)/shard_map/ppermute | solution.py:414
  57.2 2.8 %collective-permute-start.20 = (f32[4,128]{1,0:T(4,128)S(1)}, f32[4,128]{1,0:T(4,128)S(1)}, u32[]{:S(2)}, u32[]{:S(2)}) collective-permute-start(f32[4,128]{1,0:T(4,128)S(1)} %slice_bitcast_fusion.4), channel_id=1, source_target_pairs={{0,1},{1,0},{2,3},{3,2},{4,5},{5,4},{6,7},{7,6},{8,9},{9,8},{10,11... | collective-permute-start | bytes 6152 | tf_op jit(solution)/shard_map/ppermute | solution.py:458
  85.5 4.5 %collective-permute-start.21 = (f32[3,128,128]{2,1,0:T(8,128)S(1)}, f32[3,128,128]{2,1,0:T(8,128)S(1)}, u32[]{:S(2)}, u32[]{:S(2)}) collective-permute-start(f32[3,128,128]{2,1,0:T(8,128)S(1)} %get-tuple-element.151), channel_id=1, source_target_pairs={{0,1},{1,3},{2,0},{3,2},{4,5},{5,7},{6,4},{7,6},{8,9},{9,11},{10,8... | collective-permute-start | bytes 589832 | tf_op jit(solution)/shard_map/ppermute | solution.py:419
  85.9 10.0 %collective-permute-start.22 = (f32[3,128,128]{2,1,0:T(8,128)S(1)}, f32[3,128,128]{2,1,0:T(8,128)S(1)}, u32[]{:S(2)}, u32[]{:S(2)}) collective-permute-start(f32[3,128,128]{2,1,0:T(8,128)S(1)} %get-tuple-element.152), channel_id=1, source_target_pairs={{0,2},{1,0},{2,3},{3,1},{4,6},{5,4},{6,7},{7,5},{8,10},{9,8},{10,1... | collective-permute-start | bytes 589832 | tf_op jit(solution)/shard_map/ppermute | solution.py:419
  88.4 8.5 %collective-permute-start.24 = (f32[4,128,128]{2,1,0:T(8,128)S(1)}, f32[4,128,128]{2,1,0:T(8,128)S(1)}, u32[]{:S(2)}, u32[]{:S(2)}) collective-permute-start(f32[4,128,128]{2,1,0:T(8,128)S(1)} %get-tuple-element.154), channel_id=1, source_target_pairs={{0,32},{1,33},{2,34},{3,35},{4,36},{5,37},{6,38},{7,39},{8,40},{9,... | collective-permute-start | bytes 786440 | tf_op jit(solution)/shard_map/ppermute | solution.py:419
  90.0 5.7 %copy-start.4 = (f32[3,128,128]{2,1,0:T(8,128)}, f32[3,128,128]{2,1,0:T(8,128)S(1)}, u32[]{:S(2)}) copy-start(f32[3,128,128]{2,1,0:T(8,128)S(1)} %collective-permute-done.21) | copy-start | bytes 589828
  90.1 11.8 %collective-permute-start.28 = (f32[3,128,128]{2,1,0:T(8,128)S(1)}, f32[3,128,128]{2,1,0:T(8,128)S(1)}, u32[]{:S(2)}, u32[]{:S(2)}) collective-permute-start(f32[3,128,128]{2,1,0:T(8,128)S(1)} %pad_maximum_fusion.18), channel_id=1, source_target_pairs={{0,2},{1,0},{2,3},{3,1},{4,6},{5,4},{6,7},{7,5},{8,10},{9,8},{10,1... | collective-permute-start | bytes 589832 | tf_op jit(solution)/shard_map/ppermute | solution.py:419
  95.8 11.9 %collective-permute-start.27 = (f32[4,128,128]{2,1,0:T(8,128)S(1)}, f32[4,128,128]{2,1,0:T(8,128)S(1)}, u32[]{:S(2)}, u32[]{:S(2)}) collective-permute-start(f32[4,128,128]{2,1,0:T(8,128)S(1)} %pad_maximum_fusion.17), channel_id=1, source_target_pairs={{0,1},{1,3},{2,0},{3,2},{4,5},{5,7},{6,4},{7,6},{8,9},{9,11},{10,8... | collective-permute-start | bytes 786440 | tf_op jit(solution)/shard_map/ppermute | solution.py:419
  96.8 12.5 %collective-permute-start.23 = (f32[4,128,128]{2,1,0:T(8,128)S(1)}, f32[4,128,128]{2,1,0:T(8,128)S(1)}, u32[]{:S(2)}, u32[]{:S(2)}) collective-permute-start(f32[4,128,128]{2,1,0:T(8,128)S(1)} %maximum_add_fusion), channel_id=1, source_target_pairs={{0,32},{1,33},{2,34},{3,35},{4,36},{5,37},{6,38},{7,39},{8,40},{9,... | collective-permute-start | bytes 786440 | tf_op jit(solution)/shard_map/ppermute | solution.py:419
  97.0 8.8 %collective-permute-start.26 = (f32[2,128,128]{2,1,0:T(8,128)S(1)}, f32[2,128,128]{2,1,0:T(8,128)S(1)}, u32[]{:S(2)}, u32[]{:S(2)}) collective-permute-start(f32[2,128,128]{2,1,0:T(8,128)S(1)} %get-tuple-element.204), channel_id=1, source_target_pairs={{0,28},{1,29},{2,30},{3,31},{4,0},{5,1},{6,2},{7,3},{8,4},{9,5},{1... | collective-permute-start | bytes 393224 | tf_op jit(solution)/shard_map/ppermute | solution.py:419
  98.9 8.8 %collective-permute-start.25 = (f32[2,128,128]{2,1,0:T(8,128)S(1)}, f32[2,128,128]{2,1,0:T(8,128)S(1)}, u32[]{:S(2)}, u32[]{:S(2)}) collective-permute-start(f32[2,128,128]{2,1,0:T(8,128)S(1)} %get-tuple-element.205), channel_id=1, source_target_pairs={{0,4},{1,5},{2,6},{3,7},{4,8},{5,9},{6,10},{7,11},{8,12},{9,13},{1... | collective-permute-start | bytes 393224 | tf_op jit(solution)/shard_map/ppermute | solution.py:419

commit v2 on v1

--- a/solution.py
+++ b/solution.py
@@ -443,10 +443,11 @@
     beside = give_back(Z, beside)
     beside_back = give_back(Z_BACK, beside_back)
     sides = [beside[1:2], beside_back[1:2], beside[2:3], beside_back[2:3]]
-    x = give_back(X, x + jnp.concatenate(sides, 0))
-    beside, z, corner_back, z_back, corner = lax.optimization_barrier(
-        (beside, z, corner_back, z_back, corner)
+    x = x + jnp.concatenate(sides, 0)
+    x, z, corner_back, z_back, corner = lax.optimization_barrier(
+        (x, z, corner_back, z_back, corner)
     )
+    x = give_back(X, x)
     z = give_back(Z, jnp.concatenate([z, corner_back], 0))
     z_back = give_back(Z_BACK, jnp.concatenate([z_back, corner], 0))
     y = give_back(Y, y + xy[0:2] + jnp.concatenate([beside[0:1], beside_back[0:1]], 0))
@@ -471,7 +472,8 @@
     v, corner_v = left_products(corner_rows, own_u, local_m)
     *unit, so_far = unit_products(rows, row_data, own_u, parts[1], parts[2], parts[4], v)
 
-    corner_v, _ = lax.optimization_barrier((corner_v, parts[1]))
+    corner_v, x, z, z_back = lax.optimization_barrier((corner_v, parts[1], parts[4], parts[6]))
+    parts = (parts[0], x, *parts[2:4], z, parts[5], z_back, parts[7])
     corner_v = jnp.concatenate(corners(corner_v), 0)
 
     def usual(ends, rows, row_data, so_far, v, corner_v, *parts):

time: 112 us -> 110 us (0.982)
  waiting for transfers between devices: 17.1 us -> 27.9 us
  starting transfers between devices: 37.7 us -> 27 us
  local copies, waits for them, and re-layouts: 8.55 us -> 7.02 us
  blocking collectives: 22.1 us -> 20.9 us
    ppermute x10, waiting for transfers between devices: 8.83 us -> 16.9 us  [fetch(): return lax.ppermute(jnp.concatenate(blocks, 0), AXES, route)]
    ppermute x10, starting transfers between devices: 23.6 us -> 16.6 us  [fetch(): return lax.ppermute(jnp.concatenate(blocks, 0), AXES, route)]
    ppermute x8, starting transfers between devices: 12.2 us -> 9.3 us  [give_back(): return lax.ppermute(block, AXES, route)]
    ppermute x8, waiting for transfers between devices: 7.45 us -> 10.2 us  [give_back(): return lax.ppermute(block, AXES, route)]
    all_to_all x1, blocking collectives: 14.7 us -> 13.5 us  [over_all(): lax.all_to_all(copies, 'kyz', 0, 0, axis_index_groups=one_core)]
    unnamed x9 -> x7, local copies, waits for them, and re-layouts: 3.9 us -> 3.9 us
  transfers between devices with their start and end apart: 19 -> 19, of which waited for: 7 -> 7; matrix products, arithmetic and copies ran while one was open for 7% -> 6% of each run, Pallas kernels for 9% -> 9%
where the time goes in v2:
time: 110 us; the launch traced here: 109 us
  waiting for transfers between devices  27.9 us (25%)
  starting transfers between devices  27 us (25%)
  blocking collectives  20.9 us (19%)
  Pallas kernels  19.7 us (18%)
  local copies, waits for them, and re-layouts  7.02 us (6%)
  between operations  3.96 us (4%)
  other arithmetic  2.03 us (2%)
    ppermute x10, waiting for transfers between devices, fetch(): return lax.ppermute(jnp.concatenate(blocks, 0), AXES, route)  16.9 us
    ppermute x10, starting transfers between devices, fetch(): return lax.ppermute(jnp.concatenate(blocks, 0), AXES, route)  16.6 us
    all_to_all x1, blocking collectives, over_all(): lax.all_to_all(copies, 'kyz', 0, 0, axis_index_groups=one_core)  13.5 us
    ppermute x8, waiting for transfers between devices, give_back(): return lax.ppermute(block, AXES, route)  10.2 us
    ppermute x8, starting transfers between devices, give_back(): return lax.ppermute(block, AXES, route)  9.3 us
    pallas_call x2, Pallas kernels, product_call(): pl.pallas_call(kernel, in_specs=[SMEM] * len(tables) + [VMEM] * len(array...  8.35 us
    all_to_all x1, blocking collectives, over_all(): return lax.all_to_all(copies, 'kx', 0, 0)  7.42 us
    pallas_call x1, Pallas kernels, left_products(): pl.pallas_call(left_kernel, grid=(4,), in_specs=[SMEM, pl.BlockSpec((1, 2...  5.14 us
  transfers between devices with their start and end apart: 19, of which 7 were waited for; matrix products, arithmetic and copies ran while one was open for 6% of the time, Pallas kernels for 9%

profile of v2, /device:TPU:1, one launch (start us, length us, event | category | flops | bytes accessed | tf_op | source)
XLA Modules:
  0.0 108.7 jit_solution(8504664080757103484)
XLA Ops:
  0.6 4.7 %collective-permute-start.10 = (f32[4,2,128,128]{3,2,1,0:T(8,128)}, f32[4,2,128,128]{3,2,1,0:T(8,128)S(1)}, u32[]{:S(2)}, u32[]{:S(2)}) collective-permute-start(f32[4,2,128,128]{3,2,1,0:T(8,128)} %bitcast.21), channel_id=1, source_target_pairs={{32,0},{33,1},{34,2},{35,3},{36,4},{37,5},{38,6},{39,7},{40,8},{41... | collective-permute-start | bytes 1572872 | tf_op jit(solution)/shard_map/ppermute | solution.py:414
  6.3 1.4 %collective-permute-start.13 = (f32[1,2,128,128]{3,2,1,0:T(8,128)S(1)}, f32[1,2,128,128]{3,2,1,0:T(8,128)}, u32[]{:S(2)}, u32[]{:S(2)}) collective-permute-start(f32[1,2,128,128]{3,2,1,0:T(8,128)S(1)} %slice.171), channel_id=1, source_target_pairs={{2,0},{0,1},{3,2},{1,3},{6,4},{4,5},{7,6},{5,7},{10,8},{8,9},{11,1... | collective-permute-start | bytes 393224 | tf_op jit(solution)/shard_map/ppermute | solution.py:414
  9.8 2.7 %collective-permute-start.14 = (f32[2,2,128,128]{3,2,1,0:T(8,128)S(1)}, f32[2,2,128,128]{3,2,1,0:T(8,128)S(1)}, u32[]{:S(2)}, u32[]{:S(2)}) collective-permute-start(f32[2,2,128,128]{3,2,1,0:T(8,128)S(1)} %get-tuple-element.208), channel_id=1, source_target_pairs={{28,0},{29,1},{30,2},{31,3},{0,4},{1,5},{2,6},{3,7},{4,8},{5,9},{6... | collective-permute-start | bytes 786440 | tf_op jit(solution)/shard_map/ppermute | solution.py:414
  12.5 4.9 %collective-permute-start.11 = (f32[2,2,128,128]{3,2,1,0:T(8,128)S(1)}, f32[2,2,128,128]{3,2,1,0:T(8,128)S(1)}, u32[]{:S(2)}, u32[]{:S(2)}) collective-permute-start(f32[2,2,128,128]{3,2,1,0:T(8,128)S(1)} %get-tuple-element.209), channel_id=1, source_target_pairs={{4,0},{5,1},{6,2},{7,3},{8,4},{9,5},{10,6},{11,7},{12,8},{13,9},{1... | collective-permute-start | bytes 786440 | tf_op jit(solution)/shard_map/ppermute | solution.py:414
  17.5 1.4 %copy.10.offsets = s32[6,3]{1,0:T(8,128)} copy(s32[6,3]{0,1:T(4,128)} %param.9) | data formatting | bytes 144 | tf_op args[2]
  18.8 1.9 %make_rows.1 = (s32[6]{0:T(128)S(1)}, s32[4]{0:T(128)}, s32[2,3,4]{2,1,0:T(4,128)S(1)}, f32[6,4]{1,0:T(8,128)S(1)}, s32[1]{0:T(128)}) custom-call(s32[6,3]{1,0:T(8,128)} %copy.10.offsets, f32[6]{0:T(128)} %weights.1, f32[3,3]{1,0:T(4,128)} %basis.1), custom_call_target="tpu_custom_call" | custom-call | tf_op jit(solution)/shard_map/make_rows/pallas_call | solution.py:162
  20.8 1.9 %copy-done = f32[1,1,2,2,6,2,128,128]{7,6,5,4,3,2,1,0:T(8,128)S(1)} copy-done((f32[1,1,2,2,6,2,128,128]{7,6,5,4,3,2,1,0:T(8,128)S(1)}, f32[1,1,2,2,6,2,128,128]{7,6,5,4,3,2,1,0:T(8,128)}, u32[]{:S(2)}) %copy-start) | copy-done | bytes 3145752
  23.3 5.1 %left_products.1 = (f32[4,6,2,128,128]{4,3,2,1,0:T(8,128)}, f32[4,2,128,128]{3,2,1,0:T(8,128)S(1)}) custom-call(s32[4]{0:T(128)S(1)} %copy-done.1, f32[4,2,128,128]{3,2,1,0:T(8,128)} %bitcast.24, f32[4,6,2,128,128]{4,3,2,1,0:T(8,128)S(1)} %bitcast.20), custom_call_target="tpu_custom_call" | custom-call | flops 4294967296 | bytes 8388608 | tf_op jit(solution)/shard_map/left_products/pallas_call | solution.py:186
  29.1 6.8 %collective-permute-done.14 = f32[2,2,128,128]{3,2,1,0:T(8,128)S(1)} collective-permute-done((f32[2,2,128,128]{3,2,1,0:T(8,128)S(1)}, f32[2,2,128,128]{3,2,1,0:T(8,128)S(1)}, u32[]{:S(2)}, u32[]{:S(2)}) %collective-permute-start.14) | collective-permute-done | bytes 262176 | tf_op jit(solution)/shard_map/ppermute | solution.py:414
  36.2 1.9 %collective-permute-start.16 = (f32[3,2,128,128]{3,2,1,0:T(8,128)S(1)}, f32[3,2,128,128]{3,2,1,0:T(8,128)}, u32[]{:S(2)}, u32[]{:S(2)}) collective-permute-start(f32[3,2,128,128]{3,2,1,0:T(8,128)S(1)} %pad_maximum_fusion.15), channel_id=1, source_target_pairs={{1,0},{3,1},{0,2},{2,3},{5,4},{7,5},{4,6},{6,7},{9,8},{11,9},{8,10... | collective-permute-start | bytes 1179656 | tf_op jit(solution)/shard_map/ppermute | solution.py:414
  38.9 3.3 %unit_products.1 = (f32[12,2,128,128]{3,2,1,0:T(8,128)S(1)}, f32[2,3,4,128]{3,2,1,0:T(4,128)S(1)}, f32[3,4,128]{2,1,0:T(4,128)S(1)}, f32[4,128]{1,0:T(4,128)S(1)}) custom-call(s32[6]{0:T(128)S(1)} %get-tuple-element.138.rows, f32[6,4]{1,0:T(8,128)S(1)} %get-tuple-element.137.row_data, f32[4,2,128,128]{3,2,1,0:T(8,128)S(1)} %bitcast.25, ...), custom_call_target="tpu_custom_call" | custom-call | flops 4294967296 | bytes 4194304 | tf_op jit(solution)/shard_map/unit_products/pallas_call | solution.py:277
  42.2 10.0 %collective-permute-done.18 = f32[2,2,128,128]{3,2,1,0:T(8,128)S(1)} collective-permute-done((f32[2,2,128,128]{3,2,1,0:T(8,128)S(1)}, f32[2,2,128,128]{3,2,1,0:T(8,128)S(1)}, u32[]{:S(2)}, u32[]{:S(2)}) %collective-permute-start.18) | collective-permute-done | bytes 262176 | tf_op jit(solution)/shard_map/ppermute | solution.py:414
  52.3 5.3 %conditional.1 = ((f32[12,2,128,128]{3,2,1,0:T(8,128)}, f32[2,3,4,128]{3,2,1,0:T(4,128)S(1)}, f32[3,4,128]{2,1,0:T(4,128)S(1)}, f32[8,4,128]{2,1,0:T(4,128)S(1)})) conditional(s32[]{:T(128)} %bitcast.9, (s32[2,3,4]{2,1,0:T(4,128)S(1)}, s32[6]{0:T(128)S(1)}, f32[6,4]{1,0:T(8,128)S(1)}, f32[4,128]{1,0:T(4,128)S(1)}, f32[4,2,128,128]{3,2,1,0:T(8,128)S(1)}, ...), branch_computations={%region_0.0_spmd, %region_1.0_spmd} | conditional | flops 4300406784 | bytes 144704064 | solution.py:490
  52.5 5.1 %diagonal_products.2 = (f32[12,2,128,128]{3,2,1,0:T(8,128)}, f32[2,3,4,128]{3,2,1,0:T(4,128)S(1)}, f32[3,4,128]{2,1,0:T(4,128)S(1)}, f32[8,4,128]{2,1,0:T(4,128)S(1)}) custom-call(s32[2,3,4]{2,1,0:T(4,128)S(1)} %get-tuple-element.70.ends, s32[6]{0:T(128)S(1)} %get-tuple-element.71.rows, f32[6,4]{1,0:T(8,128)S(1)} %get-tuple-element.72.row_data, ...), custom_call_target="tpu_custom_call" | custom-call | flops 4294967296 | bytes 4194304 | tf_op jit(solution)/shard_map/cond/branch_0_fun/diagonal_products/pallas_call | solution.py:277
  59.6 13.5 %all_to_all.10 = f32[16,4,128]{2,1,0:T(4,128)S(1)} all-to-all(f32[16,4,128]{2,1,0:T(4,128)S(1)} %broadcast_in_dim.4), channel_id=1, replica_groups={{0,2,4,6,8,10,12,14,16,18,20,22,24,26,28,30},{1,3,5,7,9,11,13,15,17,19,..., dimensions={0} | all-to-all | bytes 65536 | tf_op jit(solution)/shard_map/all_to_all | solution.py:462
  73.1 7.4 %all_to_all.11.got_ref = f32[8,4,128]{2,1,0:T(4,128)S(1)} all-to-all(f32[8,4,128]{2,1,0:T(4,128)S(1)} %broadcast_in_dim.5), channel_id=1, replica_groups=mesh['kx'=8,'kyz'=32] {'kx'}, dimensions={0} | all-to-all | bytes 32768 | tf_op jit(solution)/shard_map/all_to_all | solution.py:464
  80.5 3.3 %pair_terms.1 = (f32[4,128]{1,0:T(4,128)S(1)}, f32[4,128,128]{2,1,0:T(8,128)S(1)}, f32[4,128,128]{2,1,0:T(8,128)S(1)}, f32[2,128,128]{2,1,0:T(8,128)S(1)}, f32[4...) custom-call(s32[2,3,4]{2,1,0:T(4,128)S(1)} %get-tuple-element.136.en, ...), custom_call_target="tpu_custom_call" | custom-call | flops 16777216 | bytes 8388608 | tf_op jit(solution)/shard_map/pair_terms/pallas_call | solution.py:372
  84.2 2.8 %collective-permute-start.22 = (f32[3,128,128]{2,1,0:T(8,128)S(1)}, f32[3,128,128]{2,1,0:T(8,128)S(1)}, u32[]{:S(2)}, u32[]{:S(2)}) collective-permute-start(f32[3,128,128]{2,1,0:T(8,128)S(1)} %get-tuple-element.158), channel_id=1, source_target_pairs={{0,2},{1,0},{2,3},{3,1},{4,6},{5,4},{6,7},{7,5},{8,10},{9,8},{10,1... | collective-permute-start | bytes 589832 | tf_op jit(solution)/shard_map/ppermute | solution.py:419
  88.7 2.3 %collective-permute-done.22 = f32[3,128,128]{2,1,0:T(8,128)S(1)} collective-permute-done((f32[3,128,128]{2,1,0:T(8,128)S(1)}, f32[3,128,128]{2,1,0:T(8,128)S(1)}, u32[]{:S(2)}, u32[]{:S(2)}) %collective-permute-start.22) | collective-permute-done | bytes 196640 | tf_op jit(solution)/shard_map/ppermute | solution.py:419
  91.1 2.2 %collective-permute-start.28 = (f32[3,128,128]{2,1,0:T(8,128)S(1)}, f32[3,128,128]{2,1,0:T(8,128)S(1)}, u32[]{:S(2)}, u32[]{:S(2)}) collective-permute-start(f32[3,128,128]{2,1,0:T(8,128)S(1)} %pad_maximum_fusion.18), channel_id=1, source_target_pairs={{0,2},{1,0},{2,3},{3,1},{4,6},{5,4},{6,7},{7,5},{8,10},{9,8},{10,1... | collective-permute-start | bytes 589832 | tf_op jit(solution)/shard_map/ppermute | solution.py:419
  93.8 1.2 %collective-permute-done.24 = f32[4,128,128]{2,1,0:T(8,128)S(1)} collective-permute-done((f32[4,128,128]{2,1,0:T(8,128)S(1)}, f32[4,128,128]{2,1,0:T(8,128)S(1)}, u32[]{:S(2)}, u32[]{:S(2)}) %collective-permute-start.24) | collective-permute-done | bytes 262176 | tf_op jit(solution)/shard_map/ppermute | solution.py:419
  96.1 2.0 %collective-permute-start.25 = (f32[2,128,128]{2,1,0:T(8,128)S(1)}, f32[2,128,128]{2,1,0:T(8,128)S(1)}, u32[]{:S(2)}, u32[]{:S(2)}) collective-permute-start(f32[2,128,128]{2,1,0:T(8,128)S(1)} %get-tuple-element.211), channel_id=1, source_target_pairs={{0,4},{1,5},{2,6},{3,7},{4,8},{5,9},{6,10},{7,11},{8,12},{9,13},{1... | collective-permute-start | bytes 393224 | tf_op jit(solution)/shard_map/ppermute | solution.py:419
  100.0 3.3 %collective-permute-done.26.y_back_ref = f32[2,128,128]{2,1,0:T(8,128)S(1)} collective-permute-done((f32[2,128,128]{2,1,0:T(8,128)S(1)}, f32[2,128,128]{2,1,0:T(8,128)S(1)}, u32[]{:S(2)}, u32[]{:S(2)}) %collective-permute-start.26) | collective-permute-done | bytes 131104 | tf_op jit(solution)/shard_map/ppermute | solution.py:419
  103.2 3.4 %collective-permute-done.25.y_ref = f32[2,128,128]{2,1,0:T(8,128)S(1)} collective-permute-done((f32[2,128,128]{2,1,0:T(8,128)S(1)}, f32[2,128,128]{2,1,0:T(8,128)S(1)}, u32[]{:S(2)}, u32[]{:S(2)}) %collective-permute-start.25) | collective-permute-done | bytes 131104 | tf_op jit(solution)/shard_map/ppermute | solution.py:419
  (53 shorter events, 12.0 us)
Async XLA Ops:
  0.6 35.4 %collective-permute-start.10 = (f32[4,2,128,128]{3,2,1,0:T(8,128)}, f32[4,2,128,128]{3,2,1,0:T(8,128)S(1)}, u32[]{:S(2)}, u32[]{:S(2)}) collective-permute-start(f32[4,2,128,128]{3,2,1,0:T(8,128)} %bitcast.21), channel_id=1, source_target_pairs={{32,0},{33,1},{34,2},{35,3},{36,4},{37,5},{38,6},{39,7},{40,8},{41... | collective-permute-start | bytes 1572872 | tf_op jit(solution)/shard_map/ppermute | solution.py:414
  6.3 31.8 %collective-permute-start.13 = (f32[1,2,128,128]{3,2,1,0:T(8,128)S(1)}, f32[1,2,128,128]{3,2,1,0:T(8,128)}, u32[]{:S(2)}, u32[]{:S(2)}) collective-permute-start(f32[1,2,128,128]{3,2,1,0:T(8,128)S(1)} %slice.171), channel_id=1, source_target_pairs={{2,0},{0,1},{3,2},{1,3},{6,4},{4,5},{7,6},{5,7},{10,8},{8,9},{11,1... | collective-permute-start | bytes 393224 | tf_op jit(solution)/shard_map/ppermute | solution.py:414
  8.7 29.5 %collective-permute-start.12 = (f32[2,2,128,128]{3,2,1,0:T(8,128)S(1)}, f32[2,2,128,128]{3,2,1,0:T(8,128)}, u32[]{:S(2)}, u32[]{:S(2)}) collective-permute-start(f32[2,2,128,128]{3,2,1,0:T(8,128)S(1)} %slice.137), channel_id=1, source_target_pairs={{1,0},{3,1},{0,2},{2,3},{5,4},{7,5},{4,6},{6,7},{9,8},{11,9},{8,10... | collective-permute-start | bytes 786440 | tf_op jit(solution)/shard_map/ppermute | solution.py:414
  9.8 26.0 %collective-permute-start.14 = (f32[2,2,128,128]{3,2,1,0:T(8,128)S(1)}, f32[2,2,128,128]{3,2,1,0:T(8,128)S(1)}, u32[]{:S(2)}, u32[]{:S(2)}) collective-permute-start(f32[2,2,128,128]{3,2,1,0:T(8,128)S(1)} %get-tuple-element.208), channel_id=1, source_target_pairs={{28,0},{29,1},{30,2},{31,3},{0,4},{1,5},{2,6},{3,7},{4,8},{5,9},{6... | collective-permute-start | bytes 786440 | tf_op jit(solution)/shard_map/ppermute | solution.py:414
  12.5 23.3 %collective-permute-start.11 = (f32[2,2,128,128]{3,2,1,0:T(8,128)S(1)}, f32[2,2,128,128]{3,2,1,0:T(8,128)S(1)}, u32[]{:S(2)}, u32[]{:S(2)}) collective-permute-start(f32[2,2,128,128]{3,2,1,0:T(8,128)S(1)} %get-tuple-element.209), channel_id=1, source_target_pairs={{4,0},{5,1},{6,2},{7,3},{8,4},{9,5},{10,6},{11,7},{12,8},{13,9},{1... | collective-permute-start | bytes 786440 | tf_op jit(solution)/shard_map/ppermute | solution.py:414
  20.7 1.9 %copy-start = (f32[1,1,2,2,6,2,128,128]{7,6,5,4,3,2,1,0:T(8,128)S(1)}, f32[1,1,2,2,6,2,128,128]{7,6,5,4,3,2,1,0:T(8,128)}, u32[]{:S(2)}) copy-start(f32[1,1,2,2,6,2,128,128]{7,6,5,4,3,2,1,0:T(8,128)} %param.7) | copy-start | bytes 9437188
  22.6 0.7 copy-start.1
  35.9 3.0 %copy-start.3 = (f32[1,1,2,2,2,128,128]{6,5,4,3,2,1,0:T(8,128)S(1)}, f32[1,1,2,2,2,128,128]{6,5,4,3,2,1,0:T(8,128)}, u32[]{:S(2)}) copy-start(f32[1,1,2,2,2,128,128]{6,5,4,3,2,1,0:T(8,128)} %param.8) | copy-start | bytes 1572868
  35.9 16.3 %collective-permute-start.15 = (f32[4,2,128,128]{3,2,1,0:T(8,128)S(1)}, f32[4,2,128,128]{3,2,1,0:T(8,128)}, u32[]{:S(2)}, u32[]{:S(2)}) collective-permute-start(f32[4,2,128,128]{3,2,1,0:T(8,128)S(1)} %pad_maximum_fusion.13), channel_id=1, source_target_pairs={{32,0},{33,1},{34,2},{35,3},{36,4},{37,5},{38,6},{39,7},{40,8},{41... | collective-permute-start | bytes 1572872 | tf_op jit(solution)/shard_map/ppermute | solution.py:414
  36.2 16.1 %collective-permute-start.16 = (f32[3,2,128,128]{3,2,1,0:T(8,128)S(1)}, f32[3,2,128,128]{3,2,1,0:T(8,128)}, u32[]{:S(2)}, u32[]{:S(2)}) collective-permute-start(f32[3,2,128,128]{3,2,1,0:T(8,128)S(1)} %pad_maximum_fusion.15), channel_id=1, source_target_pairs={{1,0},{3,1},{0,2},{2,3},{5,4},{7,5},{4,6},{6,7},{9,8},{11,9},{8,10... | collective-permute-start | bytes 1179656 | tf_op jit(solution)/shard_map/ppermute | solution.py:414
  38.1 14.2 %collective-permute-start.17 = (f32[3,2,128,128]{3,2,1,0:T(8,128)S(1)}, f32[3,2,128,128]{3,2,1,0:T(8,128)}, u32[]{:S(2)}, u32[]{:S(2)}) collective-permute-start(f32[3,2,128,128]{3,2,1,0:T(8,128)S(1)} %pad_maximum_fusion.16), channel_id=1, source_target_pairs={{2,0},{0,1},{3,2},{1,3},{6,4},{4,5},{7,6},{5,7},{10,8},{8,9},{11,1... | collective-permute-start | bytes 1179656 | tf_op jit(solution)/shard_map/ppermute | solution.py:414
  38.2 14.0 %collective-permute-start.18 = (f32[2,2,128,128]{3,2,1,0:T(8,128)S(1)}, f32[2,2,128,128]{3,2,1,0:T(8,128)S(1)}, u32[]{:S(2)}, u32[]{:S(2)}) collective-permute-start(f32[2,2,128,128]{3,2,1,0:T(8,128)S(1)} %get-tuple-element.204), channel_id=1, source_target_pairs={{2,0},{0,1},{3,2},{1,3},{6,4},{4,5},{7,6},{5,7},{10,8},{8,9},{11,1... | collective-permute-start | bytes 786440 | tf_op jit(solution)/shard_map/ppermute | solution.py:414
  38.5 13.7 %collective-permute-start.19 = (f32[2,2,128,128]{3,2,1,0:T(8,128)S(1)}, f32[2,2,128,128]{3,2,1,0:T(8,128)S(1)}, u32[]{:S(2)}, u32[]{:S(2)}) collective-permute-start(f32[2,2,128,128]{3,2,1,0:T(8,128)S(1)} %get-tuple-element.205), channel_id=1, source_target_pairs={{1,0},{3,1},{0,2},{2,3},{5,4},{7,5},{4,6},{6,7},{9,8},{11,9},{8,10... | collective-permute-start | bytes 786440 | tf_op jit(solution)/shard_map/ppermute | solution.py:414
  57.6 2.0 %collective-permute-start.20 = (f32[4,128]{1,0:T(4,128)S(1)}, f32[4,128]{1,0:T(4,128)S(1)}, u32[]{:S(2)}, u32[]{:S(2)}) collective-permute-start(f32[4,128]{1,0:T(4,128)S(1)} %slice_bitcast_fusion.4), channel_id=1, source_target_pairs={{0,1},{1,0},{2,3},{3,2},{4,5},{5,4},{6,7},{7,6},{8,9},{9,8},{10,11... | collective-permute-start | bytes 6152 | tf_op jit(solution)/shard_map/ppermute | solution.py:459
  83.9 4.8 %collective-permute-start.21 = (f32[3,128,128]{2,1,0:T(8,128)S(1)}, f32[3,128,128]{2,1,0:T(8,128)S(1)}, u32[]{:S(2)}, u32[]{:S(2)}) collective-permute-start(f32[3,128,128]{2,1,0:T(8,128)S(1)} %get-tuple-element.157), channel_id=1, source_target_pairs={{0,1},{1,3},{2,0},{3,2},{4,5},{5,7},{6,4},{7,6},{8,9},{9,11},{10,8... | collective-permute-start | bytes 589832 | tf_op jit(solution)/shard_map/ppermute | solution.py:419
  84.2 6.8 %collective-permute-start.22 = (f32[3,128,128]{2,1,0:T(8,128)S(1)}, f32[3,128,128]{2,1,0:T(8,128)S(1)}, u32[]{:S(2)}, u32[]{:S(2)}) collective-permute-start(f32[3,128,128]{2,1,0:T(8,128)S(1)} %get-tuple-element.158), channel_id=1, source_target_pairs={{0,2},{1,0},{2,3},{3,1},{4,6},{5,4},{6,7},{7,5},{8,10},{9,8},{10,1... | collective-permute-start | bytes 589832 | tf_op jit(solution)/shard_map/ppermute | solution.py:419
  87.1 8.0 %collective-permute-start.24 = (f32[4,128,128]{2,1,0:T(8,128)S(1)}, f32[4,128,128]{2,1,0:T(8,128)S(1)}, u32[]{:S(2)}, u32[]{:S(2)}) collective-permute-start(f32[4,128,128]{2,1,0:T(8,128)S(1)} %get-tuple-element.165), channel_id=1, source_target_pairs={{0,32},{1,33},{2,34},{3,35},{4,36},{5,37},{6,38},{7,39},{8,40},{9,... | collective-permute-start | bytes 786440 | tf_op jit(solution)/shard_map/ppermute | solution.py:419
  91.1 8.9 %collective-permute-start.28 = (f32[3,128,128]{2,1,0:T(8,128)S(1)}, f32[3,128,128]{2,1,0:T(8,128)S(1)}, u32[]{:S(2)}, u32[]{:S(2)}) collective-permute-start(f32[3,128,128]{2,1,0:T(8,128)S(1)} %pad_maximum_fusion.18), channel_id=1, source_target_pairs={{0,2},{1,0},{2,3},{3,1},{4,6},{5,4},{6,7},{7,5},{8,10},{9,8},{10,1... | collective-permute-start | bytes 589832 | tf_op jit(solution)/shard_map/ppermute | solution.py:419
  93.3 13.3 %collective-permute-start.27 = (f32[4,128,128]{2,1,0:T(8,128)S(1)}, f32[4,128,128]{2,1,0:T(8,128)S(1)}, u32[]{:S(2)}, u32[]{:S(2)}) collective-permute-start(f32[4,128,128]{2,1,0:T(8,128)S(1)} %pad_maximum_fusion.17), channel_id=1, source_target_pairs={{0,1},{1,3},{2,0},{3,2},{4,5},{5,7},{6,4},{7,6},{8,9},{9,11},{10,8... | collective-permute-start | bytes 786440 | tf_op jit(solution)/shard_map/ppermute | solution.py:419
  93.4 13.2 %collective-permute-start.23 = (f32[4,128,128]{2,1,0:T(8,128)S(1)}, f32[4,128,128]{2,1,0:T(8,128)S(1)}, u32[]{:S(2)}, u32[]{:S(2)}) collective-permute-start(f32[4,128,128]{2,1,0:T(8,128)S(1)} %maximum_add_fusion), channel_id=1, source_target_pairs={{0,32},{1,33},{2,34},{3,35},{4,36},{5,37},{6,38},{7,39},{8,40},{9,... | collective-permute-start | bytes 786440 | tf_op jit(solution)/shard_map/ppermute | solution.py:419
  95.1 8.2 %collective-permute-start.26 = (f32[2,128,128]{2,1,0:T(8,128)S(1)}, f32[2,128,128]{2,1,0:T(8,128)S(1)}, u32[]{:S(2)}, u32[]{:S(2)}) collective-permute-start(f32[2,128,128]{2,1,0:T(8,128)S(1)} %get-tuple-element.210), channel_id=1, source_target_pairs={{0,28},{1,29},{2,30},{3,31},{4,0},{5,1},{6,2},{7,3},{8,4},{9,5},{1... | collective-permute-start | bytes 393224 | tf_op jit(solution)/shard_map/ppermute | solution.py:419
  96.1 10.5 %collective-permute-start.25 = (f32[2,128,128]{2,1,0:T(8,128)S(1)}, f32[2,128,128]{2,1,0:T(8,128)S(1)}, u32[]{:S(2)}, u32[]{:S(2)}) collective-permute-start(f32[2,128,128]{2,1,0:T(8,128)S(1)} %get-tuple-element.211), channel_id=1, source_target_pairs={{0,4},{1,5},{2,6},{3,7},{4,8},{5,9},{6,10},{7,11},{8,12},{9,13},{1... | collective-permute-start | bytes 393224 | tf_op jit(solution)/shard_map/ppermute | solution.py:419

commit v3 on v2

--- a/solution.py
+++ b/solution.py
@@ -208,7 +208,7 @@
 
 def write_pair(p_ref, d_ref, at, left_re, left_im, right_re, right_im, b_hi, b_lo):
     a_hi, a_lo = halves(jnp.concatenate([left_re, left_im], 1))
-    slot = at % 2
+    slot = at
     block(b_hi, b_lo, slot, right_re, right_im, 1)
     made = three(a_hi, a_lo, b_hi[slot], b_lo[slot])
     eye = lax.broadcasted_iota(jnp.int32, (J, J), 0) == lax.broadcasted_iota(jnp.int32, (J, J), 1)
@@ -281,8 +281,8 @@
         out_shape=[mats(12)] + [jax.ShapeDtypeStruct(n + (J,), jnp.float32) for n in ((2, 3, 4), (3, 4), sum_shape)],
         scratch_shapes=[
             *extra,
-            pltpu.VMEM((2, 2 * J, 2 * J), jnp.bfloat16),
-            pltpu.VMEM((2, 2 * J, 2 * J), jnp.bfloat16),
+            pltpu.VMEM((12, 2 * J, 2 * J), jnp.bfloat16),
+            pltpu.VMEM((12, 2 * J, 2 * J), jnp.bfloat16),
         ],
         compiler_params=PARAMS,
         cost_estimate=pl.CostEstimate(flops=1 << 32, bytes_accessed=4 << 20, transcendentals=0),

time: 110 us -> 110 us (level)
  no operation moved by 1% of the time
where the time goes in v3:
time: 110 us; the launch traced here: 109 us
  waiting for transfers between devices  28 us (25%)
  starting transfers between devices  27 us (25%)
  blocking collectives  20.9 us (19%)
  Pallas kernels  19.4 us (18%)
  local copies, waits for them, and re-layouts  7.02 us (6%)
  between operations  3.96 us (4%)
  other arithmetic  2.03 us (2%)
    ppermute x10, waiting for transfers between devices, fetch(): return lax.ppermute(jnp.concatenate(blocks, 0), AXES, route)  17 us
    ppermute x10, starting transfers between devices, fetch(): return lax.ppermute(jnp.concatenate(blocks, 0), AXES, route)  16.6 us
    all_to_all x1, blocking collectives, over_all(): lax.all_to_all(copies, 'kyz', 0, 0, axis_index_groups=one_core)  13.5 us
    ppermute x8, waiting for transfers between devices, give_back(): return lax.ppermute(block, AXES, route)  10.2 us
    ppermute x8, starting transfers between devices, give_back(): return lax.ppermute(block, AXES, route)  9.3 us
    pallas_call x2, Pallas kernels, product_call(): pl.pallas_call(kernel, in_specs=[SMEM] * len(tables) + [VMEM] * len(array...  8.05 us
    all_to_all x1, blocking collectives, over_all(): return lax.all_to_all(copies, 'kx', 0, 0)  7.42 us
    pallas_call x1, Pallas kernels, left_products(): pl.pallas_call(left_kernel, grid=(4,), in_specs=[SMEM, pl.BlockSpec((1, 2...  5.14 us
  transfers between devices with their start and end apart: 19, of which 7 were waited for; matrix products, arithmetic and copies ran while one was open for 6% of the time, Pallas kernels for 9%

profile of v3, /device:TPU:1, one launch (start us, length us, event | category | flops | bytes accessed | tf_op | source)
XLA Modules:
  0.0 108.5 jit_solution(15032153403776606256)
XLA Ops:
  0.6 4.7 %collective-permute-start.10 = (f32[4,2,128,128]{3,2,1,0:T(8,128)}, f32[4,2,128,128]{3,2,1,0:T(8,128)S(1)}, u32[]{:S(2)}, u32[]{:S(2)}) collective-permute-start(f32[4,2,128,128]{3,2,1,0:T(8,128)} %bitcast.21), channel_id=1, source_target_pairs={{32,0},{33,1},{34,2},{35,3},{36,4},{37,5},{38,6},{39,7},{40,8},{41... | collective-permute-start | bytes 1572872 | tf_op jit(solution)/shard_map/ppermute | solution.py:414
  6.3 1.4 %collective-permute-start.13 = (f32[1,2,128,128]{3,2,1,0:T(8,128)S(1)}, f32[1,2,128,128]{3,2,1,0:T(8,128)}, u32[]{:S(2)}, u32[]{:S(2)}) collective-permute-start(f32[1,2,128,128]{3,2,1,0:T(8,128)S(1)} %slice.171), channel_id=1, source_target_pairs={{2,0},{0,1},{3,2},{1,3},{6,4},{4,5},{7,6},{5,7},{10,8},{8,9},{11,1... | collective-permute-start | bytes 393224 | tf_op jit(solution)/shard_map/ppermute | solution.py:414
  9.8 2.7 %collective-permute-start.14 = (f32[2,2,128,128]{3,2,1,0:T(8,128)S(1)}, f32[2,2,128,128]{3,2,1,0:T(8,128)S(1)}, u32[]{:S(2)}, u32[]{:S(2)}) collective-permute-start(f32[2,2,128,128]{3,2,1,0:T(8,128)S(1)} %get-tuple-element.208), channel_id=1, source_target_pairs={{28,0},{29,1},{30,2},{31,3},{0,4},{1,5},{2,6},{3,7},{4,8},{5,9},{6... | collective-permute-start | bytes 786440 | tf_op jit(solution)/shard_map/ppermute | solution.py:414
  12.5 4.9 %collective-permute-start.11 = (f32[2,2,128,128]{3,2,1,0:T(8,128)S(1)}, f32[2,2,128,128]{3,2,1,0:T(8,128)S(1)}, u32[]{:S(2)}, u32[]{:S(2)}) collective-permute-start(f32[2,2,128,128]{3,2,1,0:T(8,128)S(1)} %get-tuple-element.209), channel_id=1, source_target_pairs={{4,0},{5,1},{6,2},{7,3},{8,4},{9,5},{10,6},{11,7},{12,8},{13,9},{1... | collective-permute-start | bytes 786440 | tf_op jit(solution)/shard_map/ppermute | solution.py:414
  17.5 1.4 %copy.10.offsets = s32[6,3]{1,0:T(8,128)} copy(s32[6,3]{0,1:T(4,128)} %param.9) | data formatting | bytes 144 | tf_op args[2]
  18.8 1.9 %make_rows.1 = (s32[6]{0:T(128)S(1)}, s32[4]{0:T(128)}, s32[2,3,4]{2,1,0:T(4,128)S(1)}, f32[6,4]{1,0:T(8,128)S(1)}, s32[1]{0:T(128)}) custom-call(s32[6,3]{1,0:T(8,128)} %copy.10.offsets, f32[6]{0:T(128)} %weights.1, f32[3,3]{1,0:T(4,128)} %basis.1), custom_call_target="tpu_custom_call" | custom-call | tf_op jit(solution)/shard_map/make_rows/pallas_call | solution.py:162
  20.8 1.9 %copy-done = f32[1,1,2,2,6,2,128,128]{7,6,5,4,3,2,1,0:T(8,128)S(1)} copy-done((f32[1,1,2,2,6,2,128,128]{7,6,5,4,3,2,1,0:T(8,128)S(1)}, f32[1,1,2,2,6,2,128,128]{7,6,5,4,3,2,1,0:T(8,128)}, u32[]{:S(2)}) %copy-start) | copy-done | bytes 3145752
  23.3 5.1 %left_products.1 = (f32[4,6,2,128,128]{4,3,2,1,0:T(8,128)}, f32[4,2,128,128]{3,2,1,0:T(8,128)S(1)}) custom-call(s32[4]{0:T(128)S(1)} %copy-done.1, f32[4,2,128,128]{3,2,1,0:T(8,128)} %bitcast.24, f32[4,6,2,128,128]{4,3,2,1,0:T(8,128)S(1)} %bitcast.20), custom_call_target="tpu_custom_call" | custom-call | flops 4294967296 | bytes 8388608 | tf_op jit(solution)/shard_map/left_products/pallas_call | solution.py:186
  29.1 6.8 %collective-permute-done.14 = f32[2,2,128,128]{3,2,1,0:T(8,128)S(1)} collective-permute-done((f32[2,2,128,128]{3,2,1,0:T(8,128)S(1)}, f32[2,2,128,128]{3,2,1,0:T(8,128)S(1)}, u32[]{:S(2)}, u32[]{:S(2)}) %collective-permute-start.14) | collective-permute-done | bytes 262176 | tf_op jit(solution)/shard_map/ppermute | solution.py:414
  36.2 1.9 %collective-permute-start.16 = (f32[3,2,128,128]{3,2,1,0:T(8,128)S(1)}, f32[3,2,128,128]{3,2,1,0:T(8,128)}, u32[]{:S(2)}, u32[]{:S(2)}) collective-permute-start(f32[3,2,128,128]{3,2,1,0:T(8,128)S(1)} %pad_maximum_fusion.15), channel_id=1, source_target_pairs={{1,0},{3,1},{0,2},{2,3},{5,4},{7,5},{4,6},{6,7},{9,8},{11,9},{8,10... | collective-permute-start | bytes 1179656 | tf_op jit(solution)/shard_map/ppermute | solution.py:414
  38.9 3.1 %unit_products.1 = (f32[12,2,128,128]{3,2,1,0:T(8,128)S(1)}, f32[2,3,4,128]{3,2,1,0:T(4,128)S(1)}, f32[3,4,128]{2,1,0:T(4,128)S(1)}, f32[4,128]{1,0:T(4,128)S(1)}) custom-call(s32[6]{0:T(128)S(1)} %get-tuple-element.138.rows, f32[6,4]{1,0:T(8,128)S(1)} %get-tuple-element.137.row_data, f32[4,2,128,128]{3,2,1,0:T(8,128)S(1)} %bitcast.25, ...), custom_call_target="tpu_custom_call" | custom-call | flops 4294967296 | bytes 4194304 | tf_op jit(solution)/shard_map/unit_products/pallas_call | solution.py:277
  42.0 10.2 %collective-permute-done.18 = f32[2,2,128,128]{3,2,1,0:T(8,128)S(1)} collective-permute-done((f32[2,2,128,128]{3,2,1,0:T(8,128)S(1)}, f32[2,2,128,128]{3,2,1,0:T(8,128)S(1)}, u32[]{:S(2)}, u32[]{:S(2)}) %collective-permute-start.18) | collective-permute-done | bytes 262176 | tf_op jit(solution)/shard_map/ppermute | solution.py:414
  52.3 5.1 %conditional.1 = ((f32[12,2,128,128]{3,2,1,0:T(8,128)}, f32[2,3,4,128]{3,2,1,0:T(4,128)S(1)}, f32[3,4,128]{2,1,0:T(4,128)S(1)}, f32[8,4,128]{2,1,0:T(4,128)S(1)})) conditional(s32[]{:T(128)} %bitcast.9, (s32[2,3,4]{2,1,0:T(4,128)S(1)}, s32[6]{0:T(128)S(1)}, f32[6,4]{1,0:T(8,128)S(1)}, f32[4,128]{1,0:T(4,128)S(1)}, f32[4,2,128,128]{3,2,1,0:T(8,128)S(1)}, ...), branch_computations={%region_0.0_spmd, %region_1.0_spmd} | conditional | flops 4300406784 | bytes 144704064 | solution.py:490
  52.5 5.0 %diagonal_products.2 = (f32[12,2,128,128]{3,2,1,0:T(8,128)}, f32[2,3,4,128]{3,2,1,0:T(4,128)S(1)}, f32[3,4,128]{2,1,0:T(4,128)S(1)}, f32[8,4,128]{2,1,0:T(4,128)S(1)}) custom-call(s32[2,3,4]{2,1,0:T(4,128)S(1)} %get-tuple-element.70.ends, s32[6]{0:T(128)S(1)} %get-tuple-element.71.rows, f32[6,4]{1,0:T(8,128)S(1)} %get-tuple-element.72.row_data, ...), custom_call_target="tpu_custom_call" | custom-call | flops 4294967296 | bytes 4194304 | tf_op jit(solution)/shard_map/cond/branch_0_fun/diagonal_products/pallas_call | solution.py:277
  59.5 13.5 %all_to_all.10 = f32[16,4,128]{2,1,0:T(4,128)S(1)} all-to-all(f32[16,4,128]{2,1,0:T(4,128)S(1)} %broadcast_in_dim.4), channel_id=1, replica_groups={{0,2,4,6,8,10,12,14,16,18,20,22,24,26,28,30},{1,3,5,7,9,11,13,15,17,19,..., dimensions={0} | all-to-all | bytes 65536 | tf_op jit(solution)/shard_map/all_to_all | solution.py:462
  73.0 7.4 %all_to_all.11.got_ref = f32[8,4,128]{2,1,0:T(4,128)S(1)} all-to-all(f32[8,4,128]{2,1,0:T(4,128)S(1)} %broadcast_in_dim.5), channel_id=1, replica_groups=mesh['kx'=8,'kyz'=32] {'kx'}, dimensions={0} | all-to-all | bytes 32768 | tf_op jit(solution)/shard_map/all_to_all | solution.py:464
  80.4 3.3 %pair_terms.1 = (f32[4,128]{1,0:T(4,128)S(1)}, f32[4,128,128]{2,1,0:T(8,128)S(1)}, f32[4,128,128]{2,1,0:T(8,128)S(1)}, f32[2,128,128]{2,1,0:T(8,128)S(1)}, f32[4...) custom-call(s32[2,3,4]{2,1,0:T(4,128)S(1)} %get-tuple-element.136.en, ...), custom_call_target="tpu_custom_call" | custom-call | flops 16777216 | bytes 8388608 | tf_op jit(solution)/shard_map/pair_terms/pallas_call | solution.py:372
  84.1 2.8 %collective-permute-start.22 = (f32[3,128,128]{2,1,0:T(8,128)S(1)}, f32[3,128,128]{2,1,0:T(8,128)S(1)}, u32[]{:S(2)}, u32[]{:S(2)}) collective-permute-start(f32[3,128,128]{2,1,0:T(8,128)S(1)} %get-tuple-element.158), channel_id=1, source_target_pairs={{0,2},{1,0},{2,3},{3,1},{4,6},{5,4},{6,7},{7,5},{8,10},{9,8},{10,1... | collective-permute-start | bytes 589832 | tf_op jit(solution)/shard_map/ppermute | solution.py:419
  88.5 2.3 %collective-permute-done.22 = f32[3,128,128]{2,1,0:T(8,128)S(1)} collective-permute-done((f32[3,128,128]{2,1,0:T(8,128)S(1)}, f32[3,128,128]{2,1,0:T(8,128)S(1)}, u32[]{:S(2)}, u32[]{:S(2)}) %collective-permute-start.22) | collective-permute-done | bytes 196640 | tf_op jit(solution)/shard_map/ppermute | solution.py:419
  90.9 2.2 %collective-permute-start.28 = (f32[3,128,128]{2,1,0:T(8,128)S(1)}, f32[3,128,128]{2,1,0:T(8,128)S(1)}, u32[]{:S(2)}, u32[]{:S(2)}) collective-permute-start(f32[3,128,128]{2,1,0:T(8,128)S(1)} %pad_maximum_fusion.18), channel_id=1, source_target_pairs={{0,2},{1,0},{2,3},{3,1},{4,6},{5,4},{6,7},{7,5},{8,10},{9,8},{10,1... | collective-permute-start | bytes 589832 | tf_op jit(solution)/shard_map/ppermute | solution.py:419
  93.7 1.2 %collective-permute-done.24 = f32[4,128,128]{2,1,0:T(8,128)S(1)} collective-permute-done((f32[4,128,128]{2,1,0:T(8,128)S(1)}, f32[4,128,128]{2,1,0:T(8,128)S(1)}, u32[]{:S(2)}, u32[]{:S(2)}) %collective-permute-start.24) | collective-permute-done | bytes 262176 | tf_op jit(solution)/shard_map/ppermute | solution.py:419
  96.0 2.0 %collective-permute-start.25 = (f32[2,128,128]{2,1,0:T(8,128)S(1)}, f32[2,128,128]{2,1,0:T(8,128)S(1)}, u32[]{:S(2)}, u32[]{:S(2)}) collective-permute-start(f32[2,128,128]{2,1,0:T(8,128)S(1)} %get-tuple-element.211), channel_id=1, source_target_pairs={{0,4},{1,5},{2,6},{3,7},{4,8},{5,9},{6,10},{7,11},{8,12},{9,13},{1... | collective-permute-start | bytes 393224 | tf_op jit(solution)/shard_map/ppermute | solution.py:419
  99.8 3.3 %collective-permute-done.26.y_back_ref = f32[2,128,128]{2,1,0:T(8,128)S(1)} collective-permute-done((f32[2,128,128]{2,1,0:T(8,128)S(1)}, f32[2,128,128]{2,1,0:T(8,128)S(1)}, u32[]{:S(2)}, u32[]{:S(2)}) %collective-permute-start.26) | collective-permute-done | bytes 131104 | tf_op jit(solution)/shard_map/ppermute | solution.py:419
  103.1 3.4 %collective-permute-done.25.y_ref = f32[2,128,128]{2,1,0:T(8,128)S(1)} collective-permute-done((f32[2,128,128]{2,1,0:T(8,128)S(1)}, f32[2,128,128]{2,1,0:T(8,128)S(1)}, u32[]{:S(2)}, u32[]{:S(2)}) %collective-permute-start.25) | collective-permute-done | bytes 131104 | tf_op jit(solution)/shard_map/ppermute | solution.py:419
  (53 shorter events, 12.0 us)
Async XLA Ops:
  0.6 35.4 %collective-permute-start.10 = (f32[4,2,128,128]{3,2,1,0:T(8,128)}, f32[4,2,128,128]{3,2,1,0:T(8,128)S(1)}, u32[]{:S(2)}, u32[]{:S(2)}) collective-permute-start(f32[4,2,128,128]{3,2,1,0:T(8,128)} %bitcast.21), channel_id=1, source_target_pairs={{32,0},{33,1},{34,2},{35,3},{36,4},{37,5},{38,6},{39,7},{40,8},{41... | collective-permute-start | bytes 1572872 | tf_op jit(solution)/shard_map/ppermute | solution.py:414
  6.3 31.8 %collective-permute-start.13 = (f32[1,2,128,128]{3,2,1,0:T(8,128)S(1)}, f32[1,2,128,128]{3,2,1,0:T(8,128)}, u32[]{:S(2)}, u32[]{:S(2)}) collective-permute-start(f32[1,2,128,128]{3,2,1,0:T(8,128)S(1)} %slice.171), channel_id=1, source_target_pairs={{2,0},{0,1},{3,2},{1,3},{6,4},{4,5},{7,6},{5,7},{10,8},{8,9},{11,1... | collective-permute-start | bytes 393224 | tf_op jit(solution)/shard_map/ppermute | solution.py:414
  8.7 29.5 %collective-permute-start.12 = (f32[2,2,128,128]{3,2,1,0:T(8,128)S(1)}, f32[2,2,128,128]{3,2,1,0:T(8,128)}, u32[]{:S(2)}, u32[]{:S(2)}) collective-permute-start(f32[2,2,128,128]{3,2,1,0:T(8,128)S(1)} %slice.137), channel_id=1, source_target_pairs={{1,0},{3,1},{0,2},{2,3},{5,4},{7,5},{4,6},{6,7},{9,8},{11,9},{8,10... | collective-permute-start | bytes 786440 | tf_op jit(solution)/shard_map/ppermute | solution.py:414
  9.8 26.0 %collective-permute-start.14 = (f32[2,2,128,128]{3,2,1,0:T(8,128)S(1)}, f32[2,2,128,128]{3,2,1,0:T(8,128)S(1)}, u32[]{:S(2)}, u32[]{:S(2)}) collective-permute-start(f32[2,2,128,128]{3,2,1,0:T(8,128)S(1)} %get-tuple-element.208), channel_id=1, source_target_pairs={{28,0},{29,1},{30,2},{31,3},{0,4},{1,5},{2,6},{3,7},{4,8},{5,9},{6... | collective-permute-start | bytes 786440 | tf_op jit(solution)/shard_map/ppermute | solution.py:414
  12.5 23.3 %collective-permute-start.11 = (f32[2,2,128,128]{3,2,1,0:T(8,128)S(1)}, f32[2,2,128,128]{3,2,1,0:T(8,128)S(1)}, u32[]{:S(2)}, u32[]{:S(2)}) collective-permute-start(f32[2,2,128,128]{3,2,1,0:T(8,128)S(1)} %get-tuple-element.209), channel_id=1, source_target_pairs={{4,0},{5,1},{6,2},{7,3},{8,4},{9,5},{10,6},{11,7},{12,8},{13,9},{1... | collective-permute-start | bytes 786440 | tf_op jit(solution)/shard_map/ppermute | solution.py:414
  20.7 1.9 %copy-start = (f32[1,1,2,2,6,2,128,128]{7,6,5,4,3,2,1,0:T(8,128)S(1)}, f32[1,1,2,2,6,2,128,128]{7,6,5,4,3,2,1,0:T(8,128)}, u32[]{:S(2)}) copy-start(f32[1,1,2,2,6,2,128,128]{7,6,5,4,3,2,1,0:T(8,128)} %param.7) | copy-start | bytes 9437188
  22.6 0.7 copy-start.1
  35.9 3.0 %copy-start.3 = (f32[1,1,2,2,2,128,128]{6,5,4,3,2,1,0:T(8,128)S(1)}, f32[1,1,2,2,2,128,128]{6,5,4,3,2,1,0:T(8,128)}, u32[]{:S(2)}) copy-start(f32[1,1,2,2,2,128,128]{6,5,4,3,2,1,0:T(8,128)} %param.8) | copy-start | bytes 1572868
  35.9 16.3 %collective-permute-start.15 = (f32[4,2,128,128]{3,2,1,0:T(8,128)S(1)}, f32[4,2,128,128]{3,2,1,0:T(8,128)}, u32[]{:S(2)}, u32[]{:S(2)}) collective-permute-start(f32[4,2,128,128]{3,2,1,0:T(8,128)S(1)} %pad_maximum_fusion.13), channel_id=1, source_target_pairs={{32,0},{33,1},{34,2},{35,3},{36,4},{37,5},{38,6},{39,7},{40,8},{41... | collective-permute-start | bytes 1572872 | tf_op jit(solution)/shard_map/ppermute | solution.py:414
  36.2 16.1 %collective-permute-start.16 = (f32[3,2,128,128]{3,2,1,0:T(8,128)S(1)}, f32[3,2,128,128]{3,2,1,0:T(8,128)}, u32[]{:S(2)}, u32[]{:S(2)}) collective-permute-start(f32[3,2,128,128]{3,2,1,0:T(8,128)S(1)} %pad_maximum_fusion.15), channel_id=1, source_target_pairs={{1,0},{3,1},{0,2},{2,3},{5,4},{7,5},{4,6},{6,7},{9,8},{11,9},{8,10... | collective-permute-start | bytes 1179656 | tf_op jit(solution)/shard_map/ppermute | solution.py:414
  38.1 14.2 %collective-permute-start.17 = (f32[3,2,128,128]{3,2,1,0:T(8,128)S(1)}, f32[3,2,128,128]{3,2,1,0:T(8,128)}, u32[]{:S(2)}, u32[]{:S(2)}) collective-permute-start(f32[3,2,128,128]{3,2,1,0:T(8,128)S(1)} %pad_maximum_fusion.16), channel_id=1, source_target_pairs={{2,0},{0,1},{3,2},{1,3},{6,4},{4,5},{7,6},{5,7},{10,8},{8,9},{11,1... | collective-permute-start | bytes 1179656 | tf_op jit(solution)/shard_map/ppermute | solution.py:414
  38.2 14.0 %collective-permute-start.18 = (f32[2,2,128,128]{3,2,1,0:T(8,128)S(1)}, f32[2,2,128,128]{3,2,1,0:T(8,128)S(1)}, u32[]{:S(2)}, u32[]{:S(2)}) collective-permute-start(f32[2,2,128,128]{3,2,1,0:T(8,128)S(1)} %get-tuple-element.204), channel_id=1, source_target_pairs={{2,0},{0,1},{3,2},{1,3},{6,4},{4,5},{7,6},{5,7},{10,8},{8,9},{11,1... | collective-permute-start | bytes 786440 | tf_op jit(solution)/shard_map/ppermute | solution.py:414
  38.5 13.7 %collective-permute-start.19 = (f32[2,2,128,128]{3,2,1,0:T(8,128)S(1)}, f32[2,2,128,128]{3,2,1,0:T(8,128)S(1)}, u32[]{:S(2)}, u32[]{:S(2)}) collective-permute-start(f32[2,2,128,128]{3,2,1,0:T(8,128)S(1)} %get-tuple-element.205), channel_id=1, source_target_pairs={{1,0},{3,1},{0,2},{2,3},{5,4},{7,5},{4,6},{6,7},{9,8},{11,9},{8,10... | collective-permute-start | bytes 786440 | tf_op jit(solution)/shard_map/ppermute | solution.py:414
  57.4 2.0 %collective-permute-start.20 = (f32[4,128]{1,0:T(4,128)S(1)}, f32[4,128]{1,0:T(4,128)S(1)}, u32[]{:S(2)}, u32[]{:S(2)}) collective-permute-start(f32[4,128]{1,0:T(4,128)S(1)} %slice_bitcast_fusion.4), channel_id=1, source_target_pairs={{0,1},{1,0},{2,3},{3,2},{4,5},{5,4},{6,7},{7,6},{8,9},{9,8},{10,11... | collective-permute-start | bytes 6152 | tf_op jit(solution)/shard_map/ppermute | solution.py:459
  83.7 4.8 %collective-permute-start.21 = (f32[3,128,128]{2,1,0:T(8,128)S(1)}, f32[3,128,128]{2,1,0:T(8,128)S(1)}, u32[]{:S(2)}, u32[]{:S(2)}) collective-permute-start(f32[3,128,128]{2,1,0:T(8,128)S(1)} %get-tuple-element.157), channel_id=1, source_target_pairs={{0,1},{1,3},{2,0},{3,2},{4,5},{5,7},{6,4},{7,6},{8,9},{9,11},{10,8... | collective-permute-start | bytes 589832 | tf_op jit(solution)/shard_map/ppermute | solution.py:419
  84.1 6.8 %collective-permute-start.22 = (f32[3,128,128]{2,1,0:T(8,128)S(1)}, f32[3,128,128]{2,1,0:T(8,128)S(1)}, u32[]{:S(2)}, u32[]{:S(2)}) collective-permute-start(f32[3,128,128]{2,1,0:T(8,128)S(1)} %get-tuple-element.158), channel_id=1, source_target_pairs={{0,2},{1,0},{2,3},{3,1},{4,6},{5,4},{6,7},{7,5},{8,10},{9,8},{10,1... | collective-permute-start | bytes 589832 | tf_op jit(solution)/shard_map/ppermute | solution.py:419
  86.9 8.0 %collective-permute-start.24 = (f32[4,128,128]{2,1,0:T(8,128)S(1)}, f32[4,128,128]{2,1,0:T(8,128)S(1)}, u32[]{:S(2)}, u32[]{:S(2)}) collective-permute-start(f32[4,128,128]{2,1,0:T(8,128)S(1)} %get-tuple-element.165), channel_id=1, source_target_pairs={{0,32},{1,33},{2,34},{3,35},{4,36},{5,37},{6,38},{7,39},{8,40},{9,... | collective-permute-start | bytes 786440 | tf_op jit(solution)/shard_map/ppermute | solution.py:419
  90.9 8.9 %collective-permute-start.28 = (f32[3,128,128]{2,1,0:T(8,128)S(1)}, f32[3,128,128]{2,1,0:T(8,128)S(1)}, u32[]{:S(2)}, u32[]{:S(2)}) collective-permute-start(f32[3,128,128]{2,1,0:T(8,128)S(1)} %pad_maximum_fusion.18), channel_id=1, source_target_pairs={{0,2},{1,0},{2,3},{3,1},{4,6},{5,4},{6,7},{7,5},{8,10},{9,8},{10,1... | collective-permute-start | bytes 589832 | tf_op jit(solution)/shard_map/ppermute | solution.py:419
  93.2 13.3 %collective-permute-start.27 = (f32[4,128,128]{2,1,0:T(8,128)S(1)}, f32[4,128,128]{2,1,0:T(8,128)S(1)}, u32[]{:S(2)}, u32[]{:S(2)}) collective-permute-start(f32[4,128,128]{2,1,0:T(8,128)S(1)} %pad_maximum_fusion.17), channel_id=1, source_target_pairs={{0,1},{1,3},{2,0},{3,2},{4,5},{5,7},{6,4},{7,6},{8,9},{9,11},{10,8... | collective-permute-start | bytes 786440 | tf_op jit(solution)/shard_map/ppermute | solution.py:419
  93.3 13.2 %collective-permute-start.23 = (f32[4,128,128]{2,1,0:T(8,128)S(1)}, f32[4,128,128]{2,1,0:T(8,128)S(1)}, u32[]{:S(2)}, u32[]{:S(2)}) collective-permute-start(f32[4,128,128]{2,1,0:T(8,128)S(1)} %maximum_add_fusion), channel_id=1, source_target_pairs={{0,32},{1,33},{2,34},{3,35},{4,36},{5,37},{6,38},{7,39},{8,40},{9,... | collective-permute-start | bytes 786440 | tf_op jit(solution)/shard_map/ppermute | solution.py:419
  94.9 8.2 %collective-permute-start.26 = (f32[2,128,128]{2,1,0:T(8,128)S(1)}, f32[2,128,128]{2,1,0:T(8,128)S(1)}, u32[]{:S(2)}, u32[]{:S(2)}) collective-permute-start(f32[2,128,128]{2,1,0:T(8,128)S(1)} %get-tuple-element.210), channel_id=1, source_target_pairs={{0,28},{1,29},{2,30},{3,31},{4,0},{5,1},{6,2},{7,3},{8,4},{9,5},{1... | collective-permute-start | bytes 393224 | tf_op jit(solution)/shard_map/ppermute | solution.py:419
  96.0 10.5 %collective-permute-start.25 = (f32[2,128,128]{2,1,0:T(8,128)S(1)}, f32[2,128,128]{2,1,0:T(8,128)S(1)}, u32[]{:S(2)}, u32[]{:S(2)}) collective-permute-start(f32[2,128,128]{2,1,0:T(8,128)S(1)} %get-tuple-element.211), channel_id=1, source_target_pairs={{0,4},{1,5},{2,6},{3,7},{4,8},{5,9},{6,10},{7,11},{8,12},{9,13},{1... | collective-permute-start | bytes 393224 | tf_op jit(solution)/shard_map/ppermute | solution.py:419
